TPU v7x, 256 devices: a whole 4x4x8 slice. The times are simulated.
256 devices in a mesh: ctx: 64 (over z, x, core), tp: 4 (over y).
Axes of the slice: x: 4, y: 4, z: 8, core: 2. Of those that a mesh axis runs over, the one named last changes fastest.
Arguments:
- queries: bfloat16 [8192, 3072], P('ctx', 'tp'), may hold values from -70 to 70
- keys: bfloat16 [8192, 512], P('ctx', 'tp'), may hold values from -6 to 6
- values: bfloat16 [8192, 512], P('ctx', 'tp'), may hold values from -6 to 6
- out_grad: bfloat16 [8192, 6144], P('ctx', 'tp'), may hold values from -6 to 6
- out_weight: bfloat16 [3072, 6144], P('tp'), may hold values from -0.078125 to 0.078125
- pair_order: int32 [64], replicated, may hold values from 0 to 63, each once
Outputs:
- query_gradient: float32 [8192, 3072], P('ctx', 'tp')
- grad_keys: float32 [8192, 512], P('ctx', 'tp')
- grad_values: float32 [8192, 512], P('ctx', 'tp')
Inputs may be any that keep to these rules, and one draw needn't show every extreme that they name: A permutation: ctx index i holds the spans pair_order[i] and 127 - pair_order[i] of 64 positions, the lower one in its first 64 rows.
All inputs are finite; a program needn't handle non-finite values.
Results may differ from a plain program's by a relative error of at most 0.01.
Values may be sent and summed in bfloat16 or wider, within the bound.
No kernel may reach another device: no remote copies, remote signals or barrier semaphores. Data moves between devices by JAX's collectives and lax.ppermute only.
A program may use at most 64 MiB of HBM per device.

v0:
```python
import math

import jax
import jax.numpy as jnp
from jax import lax
from jax.sharding import PartitionSpec as P

HEAD_SIZE = 128


def position_rows(local_row, pair_ids, ctx_count, half_len):
    span_ids = jnp.where(local_row < half_len, pair_ids, 2 * ctx_count - 1 - pair_ids)
    return span_ids * half_len + local_row % half_len


def attention_scores(query_part, key_block, query_pos, key_pos, score_scale):
    scores = (
        jnp.einsum("qhd,kd->hqk", query_part, key_block, preferred_element_type=jnp.float32)
        * score_scale
    )
    return jnp.where((key_pos[None, :] <= query_pos[:, None])[None], scores, -jnp.inf)


def stat_block(states, key_block, value_block, key_pos, query_sets, score_scale):
    query_part, grads_part, query_pos = query_sets[0]

    def update(stats_state, query_part=query_part, grads_part=grads_part, query_pos=query_pos):
        running_max, denominator, weighted = stats_state
        scores = attention_scores(query_part, key_block, query_pos, key_pos, score_scale)
        dprobs = jnp.einsum(
            "qhd,kd->hqk", grads_part, value_block, preferred_element_type=jnp.float32
        )
        new_max = jnp.maximum(running_max, jnp.max(scores, axis=2))
        factor = jnp.exp(running_max - new_max)
        weights = jnp.exp(scores - new_max[:, :, None])
        return (
            new_max,
            denominator * factor + jnp.sum(weights, axis=2),
            weighted * factor + jnp.sum(weights * dprobs, axis=2),
        )

    results = [update(states[0])]
    return tuple(results)


def stat_sweep(states, key_rows, value_rows, key_pos, query_sets, score_scale, block_length):
    row_count = key_rows.shape[0]
    number_of_blocks = row_count // block_length

    def stat_advance(folded, blocks):
        return (stat_block(folded, blocks[0], blocks[1], blocks[2], query_sets, score_scale), None)

    blocks = (
        key_rows.reshape(number_of_blocks, block_length, key_rows.shape[1]),
        value_rows.reshape(number_of_blocks, block_length, value_rows.shape[1]),
        key_pos.reshape(number_of_blocks, block_length),
    )
    final, unused = lax.scan(stat_advance, states, blocks)
    return final


def grad_block(query_grads, key_block, value_block, key_pos, query_sets, finals, score_scale):
    query_part, grads_part, query_pos = query_sets[0]
    log_total, delta = finals[0]

    def compute(
        grad_state,
        query_part=query_part,
        grads_part=grads_part,
        query_pos=query_pos,
        log_total=log_total,
        delta=delta,
    ):
        scores = attention_scores(query_part, key_block, query_pos, key_pos, score_scale)
        probs = jnp.exp(scores - log_total[:, :, None])
        dprobs = jnp.einsum(
            "qhd,kd->hqk", grads_part, value_block, preferred_element_type=jnp.float32
        )
        dscores = (probs * (dprobs - delta[:, :, None])).astype(jnp.bfloat16)
        probs_low = probs.astype(jnp.bfloat16)
        grad_next = grad_state + score_scale * jnp.einsum(
            "hqk,kd->qhd", dscores, key_block, preferred_element_type=jnp.float32
        )
        key_term = score_scale * jnp.einsum(
            "hqk,qhd->kd", dscores, query_part, preferred_element_type=jnp.float32
        )
        value_term = jnp.einsum(
            "hqk,qhd->kd", probs_low, grads_part, preferred_element_type=jnp.float32
        )
        return (grad_next, key_term, value_term)

    outcome = compute(query_grads[0])
    new_grads = [outcome[0]]
    key_sum = outcome[1]
    value_sum = outcome[2]
    return (tuple(new_grads), key_sum, value_sum)


def shards(queries, keys, values, out_grad, out_weight, pair_order):
    local_rows = queries.shape[0]
    half_len = local_rows // 2
    ctx_count = lax.axis_size("ctx")
    seq_rows = local_rows * ctx_count
    head_count = queries.shape[1] // HEAD_SIZE
    score_scale = HEAD_SIZE ** (-0.5)
    ctx_slots = jnp.arange(ctx_count, dtype=jnp.int32)
    my_pair = jnp.sum(jnp.where(ctx_slots == lax.axis_index("ctx"), pair_order, 0))
    query_positions = position_rows(
        jnp.arange(local_rows, dtype=jnp.int32), my_pair, ctx_count, half_len
    )
    all_rows = jnp.arange(seq_rows, dtype=jnp.int32)
    pair_ids = jnp.sum(
        jnp.where((all_rows // local_rows)[:, None] == ctx_slots[None, :], pair_order[None, :], 0),
        axis=1,
    )
    key_positions = position_rows(all_rows % local_rows, pair_ids, ctx_count, half_len)
    whole_grad = lax.all_gather(out_grad, "tp", axis=1, tiled=True)
    projected = lax.dot_general(
        whole_grad, out_weight, (((1,), (1,)), ((), ())), preferred_element_type=jnp.float32
    )
    head_gradient = projected.astype(jnp.bfloat16)
    query_three = queries.reshape(local_rows, head_count, HEAD_SIZE)
    grads_three = head_gradient.reshape(local_rows, head_count, HEAD_SIZE)
    query_sets = ((query_three, grads_three, query_positions),)
    initial = tuple(
        (
            (
                jnp.full((head_count, query_part[0].shape[0]), -1e30, jnp.float32),
                jnp.zeros((head_count, query_part[0].shape[0]), jnp.float32),
                jnp.zeros((head_count, query_part[0].shape[0]), jnp.float32),
            )
            for query_part in query_sets
        )
    )
    gathered_keys, gathered_values = (
        lax.all_gather(keys, "ctx", axis=0, tiled=True),
        lax.all_gather(values, "ctx", axis=0, tiled=True),
    )
    block_length = math.gcd(seq_rows, 512)
    states = stat_sweep(
        initial,
        gathered_keys,
        gathered_values,
        key_positions,
        query_sets,
        score_scale,
        block_length,
    )
    finals = tuple(
        (
            (stats_state[0] + jnp.log(stats_state[1]), stats_state[2] / stats_state[1])
            for stats_state in states
        )
    )
    number_of_blocks = seq_rows // block_length

    def body_advance(query_grads, blocks):
        new_grads, key_sum, value_sum = grad_block(
            query_grads, blocks[0], blocks[1], blocks[2], query_sets, finals, score_scale
        )
        return (new_grads, (key_sum, value_sum))

    grad_init = tuple((jnp.zeros(query_part[0].shape, jnp.float32) for query_part in query_sets))
    blocks = (
        gathered_keys.reshape(number_of_blocks, block_length, HEAD_SIZE),
        gathered_values.reshape(number_of_blocks, block_length, HEAD_SIZE),
        key_positions.reshape(number_of_blocks, block_length),
    )
    query_grads, (key_terms, value_terms) = lax.scan(body_advance, grad_init, blocks)
    key_parts = key_terms.reshape(seq_rows, HEAD_SIZE)
    value_parts = value_terms.reshape(seq_rows, HEAD_SIZE)
    grad_keys, grad_values = (
        lax.psum_scatter(key_parts, "ctx", scatter_dimension=0, tiled=True),
        lax.psum_scatter(value_parts, "ctx", scatter_dimension=0, tiled=True),
    )
    query_gradient = query_grads[0].reshape(local_rows, head_count * HEAD_SIZE)
    return (query_gradient, grad_keys, grad_values)


def solution(mesh):
    return jax.shard_map(
        shards,
        mesh=mesh,
        in_specs=(
            P("ctx", "tp"),
            P("ctx", "tp"),
            P("ctx", "tp"),
            P("ctx", "tp"),
            P("tp", None),
            P(),
        ),
        out_specs=(P("ctx", "tp"), P("ctx", "tp"), P("ctx", "tp")),
        check_vma=False,
    )
```

profile of v0, /device:TPU:1, one launch (start us, length us, event | category | flops | bytes accessed | tf_op | source)
XLA Modules:
  0.0 661.3 jit_solution(15942516294141973741)
XLA Ops:
  11.8 1.3 fusion.45
  13.8 28.9 %all-gather.8.cloned.1.call-done = bf16[128,6144]{1,0:T(8,128)(2,1)} async-done(((bf16[128,1536]{1,0:T(8,128)(2,1)}), bf16[128,6144]{1,0:T(8,128)(2,1)}) %all-gather.8.cloned.1.call-update) | async-done | bytes 1572880 | tf_op jit(solution)/shard_map/all_gather | solution.py:117
  42.7 7.4 %convolution_convert_fusion = bf16[128,768]{1,0:T(8,128)(2,1)S(1)} fusion(bf16[128,6144]{1,0:T(8,128)(2,1)} %all-gather.8.cloned.1.call-done, bf16[768,6144]{1,0:T(8,128)(2,1)} %param.14), kind=kOutput, calls=%fused_computation.58 | convolution fusion | flops 1208057856 | bytes 11206656 | tf_op jit(solution)/shard_map/dot_general | solution.py:118
  50.5 72.7 %all-gather.4.cloned.1.call-done = bf16[8192,128]{1,0:T(8,128)(2,1)} async-done(((bf16[128,128]{1,0:T(8,128)(2,1)}), bf16[8192,128]{1,0:T(8,128)(2,1)}) %all-gather.4.cloned.1.call-update) | async-done | bytes 2097168 | tf_op jit(solution)/shard_map/all_gather | solution.py:136
  123.2 77.7 %all-gather.6.cloned.1.call-done = bf16[8192,128]{1,0:T(8,128)(2,1)} async-done(((bf16[128,128]{1,0:T(8,128)(2,1)}), bf16[8192,128]{1,0:T(8,128)(2,1)}) %all-gather.6.cloned.1.call-update) | async-done | bytes 2097168 | tf_op jit(solution)/shard_map/all_gather | solution.py:137
  201.0 59.4 %while.30 = (s32[]{:T(128)}, f32[6,128]{1,0:T(8,128)S(1)}, f32[6,128]{1,0:T(8,128)S(1)}, f32[6,128]{1,0:T(8,128)S(1)}, s32[16,512]{1,0:T(8,128)S(1)}, /*index=5*...) while((s32[]{:T(128)}, f32[6,128]{1,0:T(8,128)S(1)}, ...), condition=%wide.region_6.7_spmd.clone, body=%wide.region_2.6_spmd.clone.sunk | while | flops 204544512 | bytes 5567652 | solution.py:58
  201.8 1.3 fusion.86
  203.1 1.3 fusion.87
  205.5 1.3 fusion.86
  206.8 1.3 fusion.87
  209.2 1.3 fusion.86
  210.5 1.3 fusion.87
  212.9 1.3 fusion.86
  214.2 1.3 fusion.87
  216.6 1.3 fusion.86
  217.9 1.3 fusion.87
  220.3 1.3 fusion.86
  221.6 1.3 fusion.87
  224.1 1.3 fusion.86
  225.4 1.3 fusion.87
  227.8 1.3 fusion.86
  229.1 1.3 fusion.87
  231.5 1.3 fusion.86
  232.8 1.3 fusion.87
  235.2 1.3 fusion.86
  236.5 1.3 fusion.87
  238.9 1.3 fusion.86
  240.2 1.3 fusion.87
  242.6 1.3 fusion.86
  243.9 1.3 fusion.87
  246.3 1.3 fusion.86
  247.6 1.3 fusion.87
  250.0 1.3 fusion.86
  251.4 1.3 fusion.87
  253.8 1.3 fusion.86
  255.1 1.3 fusion.87
  257.5 1.3 fusion.86
  258.8 1.3 fusion.87
  260.4 110.9 %while.31 = (s32[]{:T(128)}, f32[128,6,128]{0,2,1:T(8,128)S(1)}, f32[16,512,128]{2,1,0:T(8,128)}, f32[16,512,128]{2,1,0:T(8,128)}, bf16[16,512,128]{2,1,0:T(8,12...) while((s32[]{:T(128)}, f32[128,6,128]{0,2,1:T(8,128)S(1)}, ...), condition=%wide.region_8.9_spmd.clone, body=%wide.region_7.8_spmd.clone.sunk | while | flops 506496256 | bytes 9712831 | solution.py:169
  261.2 1.4 fusion.101
  268.1 1.4 fusion.101
  275.0 1.4 fusion.101
  276.4 1.3 fusion.102
  282.0 1.4 fusion.101
  283.3 1.3 fusion.102
  288.9 1.4 fusion.101
  295.8 1.4 fusion.101
  297.2 1.3 fusion.102
  302.8 1.4 fusion.101
  309.7 1.4 fusion.101
  316.6 1.4 fusion.101
  318.0 1.3 fusion.102
  323.6 1.4 fusion.101
  325.0 1.3 fusion.102
  330.5 1.4 fusion.101
  331.9 1.3 fusion.102
  337.5 1.4 fusion.101
  344.4 1.4 fusion.101
  345.8 1.3 fusion.102
  351.3 1.4 fusion.101
  358.3 1.4 fusion.101
  365.2 1.4 fusion.101
  372.8 134.7 %reduce-scatter.5.cloned.1.call-done = f32[128,128]{1,0:T(8,128)} async-done(((f32[8192,128]{1,0:T(8,128)}), f32[128,128]{1,0:T(8,128)}) %reduce-scatter.5.cloned.1.call-update) | async-done | bytes 65552 | tf_op jit(solution)/shard_map/reduce_scatter | solution.py:174
  507.5 147.3 %reduce-scatter.3.cloned.1.call-done = f32[128,128]{1,0:T(8,128)} async-done(((f32[8192,128]{1,0:T(8,128)}), f32[128,128]{1,0:T(8,128)}) %reduce-scatter.3.cloned.1.call-update) | async-done | bytes 65552 | tf_op jit(solution)/shard_map/reduce_scatter | solution.py:173
  (243 shorter events, 102.3 us)
Async XLA Ops:
  7.2 35.6 %all-gather.8.cloned.1.call-start = ((), (), s32[]{:S(2)}) async-start(), calls=%async_computation.4 | async-start | bytes 1966080 | tf_op jit(solution)/shard_map/all_gather | solution.py:117
  7.9 115.3 %all-gather.4.cloned.1.call-start = ((), (), s32[]{:S(2)}) async-start(), calls=%async_computation.2 | async-start | bytes 2129920 | tf_op jit(solution)/shard_map/all_gather | solution.py:136
  8.6 192.3 %all-gather.6.cloned.1.call-start = ((), (), s32[]{:S(2)}) async-start(), calls=%async_computation.3 | async-start | bytes 2129920 | tf_op jit(solution)/shard_map/all_gather | solution.py:137
  9.4 498.1 %reduce-scatter.5.cloned.1.call-start = ((), (), s32[]{:S(2)}) async-start(), calls=%async_computation.6 | async-start | bytes 4259840 | tf_op jit(solution)/shard_map/reduce_scatter | solution.py:174
  371.3 283.5 %reduce-scatter.3.cloned.1.call-start = ((), (), s32[]{:S(2)}) async-start(), calls=%async_computation.5 | async-start | bytes 4259840 | tf_op jit(solution)/shard_map/reduce_scatter | solution.py:173
Sparse Core Ops, SparseCore 0:
  9.8 32.8 all-gather.7
  45.5 77.6 all-gather.3
  126.0 74.9 all-gather.5
  371.4 136.0 reduce-scatter.4
  512.6 142.1 reduce-scatter.2
where the time goes:
time: 667 us; the launch traced here: 661 us
  waiting for transfers between devices  464 us (70%)
  matrix products  146 us (22%)
  other arithmetic  31.4 us (5%)
  between operations  14.5 us (2%)
    reduce_scatter x1, waiting for transfers between devices, shards(): lax.psum_scatter(key_parts, 'ctx', scatter_dimension=0, tiled=True)  147 us
    reduce_scatter x1, waiting for transfers between devices, shards(): lax.psum_scatter(value_parts, 'ctx', scatter_dimension=0, tiled=True)  135 us
    all_gather x1, waiting for transfers between devices, shards(): lax.all_gather(values, 'ctx', axis=0, tiled=True)  77.7 us
    all_gather x1, waiting for transfers between devices, shards(): lax.all_gather(keys, 'ctx', axis=0, tiled=True)  72.7 us
    dot_general x32, matrix products, attention_scores(): jnp.einsum('qhd,kd->hqk', query_part, key_block, preferred_element_type=j...  42.6 us
    all_gather x1, waiting for transfers between devices, shards(): whole_grad = lax.all_gather(out_grad, 'tp', axis=1, tiled=True)  28.9 us
    add x33, other arithmetic, position_rows(): return span_ids * half_len + local_row % half_len  20.9 us
    dot_general x16, matrix products, update(): jnp.einsum('qhd,kd->hqk', grads_part, value_block, preferred_element_type...  20.9 us
  transfers between devices with their start and end apart: 5, of which 5 were waited for; matrix products, arithmetic and copies ran while one was open for 2% of the time, Pallas kernels for 0%

commit v1 on v0

v1 whole, which is shorter than its diff:
```python
import jax
import jax.numpy as jnp
from jax import lax
from jax.experimental import pallas as pl
from jax.experimental.pallas import tpu as pltpu
from jax.sharding import Mesh, PartitionSpec as P

HEAD = 128
HEADS = 6
SPAN = 64
SPANS = 128
ROWS = HEADS * SPAN
BLOCK = 256
PER_BLOCK = BLOCK // SPAN
STEPS = SPANS // PER_BLOCK + 1
SEQ = SPANS * SPAN
LOG2E = 1.4426950408889634
SCALE = HEAD ** -0.5
NZ, NX, NC, NY = 8, 4, 2, 4


def attention_kernel(*refs):
    meta, pair, q_ref, g_ref = refs[:4]
    chunks = refs[4:20]
    dq_ref, out_ref = refs[20:22]
    (kv, e_s, d_s, acc, stage, q_n, g_n, q_t, g_t, m_s, l_s, w_s, fac, dq_t,
     in_sem, out_sem) = refs[22:]
    z, x, c = meta[0], meta[1], meta[2]
    mine = pair[(z * NX + x) * NC + c]

    copies = []
    for a in range(16):
        dz, dc = a // 2, a % 2
        for dx in range(NX):
            who = (((z + NZ - dz) % NZ) * NX + (x + NX - dx) % NX) * NC + (c + dc) % NC
            p = pair[who]
            for half, span in ((0, p), (1, SPANS - 1 - p)):
                n = (a * NX + dx) * 2 + half
                copy = pltpu.make_async_copy(
                    chunks[a].at[dx, pl.ds(half * SPAN, SPAN), :],
                    kv.at[pl.ds(pl.multiple_of(span * SPAN, SPAN), SPAN), :],
                    in_sem.at[n],
                )
                copy.start()
                copies.append(copy)

    acc[...] = jnp.zeros_like(acc)
    dq_t[...] = jnp.zeros_like(dq_t)
    for s in range(2):
        for h in range(HEADS):
            rows = pl.ds(s * SPAN, SPAN)
            cols = pl.ds(h * HEAD, HEAD)
            q_n[s, pl.ds(h * SPAN, SPAN), :] = q_ref[rows, cols]
            g_n[s, pl.ds(h * SPAN, SPAN), :] = g_ref[rows, cols]
        q_t[s] = q_n[s].T
        g_t[s] = g_n[s].T
    for copy in copies:
        copy.wait()

    spans = (mine, SPANS - 1 - mine)
    n_low = spans[0] // PER_BLOCK + 1
    n_high = spans[1] // PER_BLOCK + 1

    def first(t, s, j, masked):
        keys = kv[pl.ds(pl.multiple_of(j * BLOCK, BLOCK), BLOCK), 0:HEAD]
        vals = kv[pl.ds(pl.multiple_of(j * BLOCK, BLOCK), BLOCK), HEAD:2 * HEAD]
        sc = jnp.dot(keys, q_t[s], preferred_element_type=jnp.float32)
        dp = jnp.dot(vals, g_t[s], preferred_element_type=jnp.float32)
        if masked:
            kp = j * BLOCK + lax.broadcasted_iota(jnp.int32, sc.shape, 0)
            qp = spans[s] * SPAN + lax.broadcasted_iota(jnp.int32, sc.shape, 1) % SPAN
            sc = jnp.where(kp <= qp, sc, -jnp.inf)
        m = jnp.max(sc, axis=0, keepdims=True)
        e = jnp.exp2((sc - m) * (SCALE * LOG2E))
        e_s[t] = e
        d_s[t] = dp
        m_s[t] = jnp.broadcast_to(m, (8, ROWS))
        l_s[t] = jnp.broadcast_to(jnp.sum(e, axis=0, keepdims=True), (8, ROWS))
        w_s[t] = jnp.broadcast_to(jnp.sum(e * dp, axis=0, keepdims=True), (8, ROWS))

    first(0, 0, n_low - 1, True)
    first(1, 1, n_high - 1, True)

    def place(t):
        low = t < n_low - 1
        s = jnp.where(low, 0, 1)
        j = jnp.where(low, t, t - (n_low - 1))
        return s, j

    def first_body(t, carry):
        s, j = place(t)
        first(t + 2, s, j, False)
        return carry

    lax.fori_loop(0, STEPS - 2, first_body, 0)

    def step_is_low(t):
        return jnp.logical_or(t == 0, jnp.logical_and(t >= 2, t - 2 < n_low - 1))

    neg = jnp.full((8, ROWS), -jnp.inf, jnp.float32)

    def max_body(t, carry):
        lo, hi = carry
        low = step_is_low(t)
        m = m_s[t]
        return (jnp.maximum(lo, jnp.where(low, m, neg)), jnp.maximum(hi, jnp.where(low, neg, m)))

    top = lax.fori_loop(0, STEPS, max_body, (neg, neg))
    zero = jnp.zeros((8, ROWS), jnp.float32)

    def sum_body(t, carry):
        l0, w0, l1, w1 = carry
        low = step_is_low(t)
        f = jnp.exp2((m_s[t] - jnp.where(low, top[0], top[1])) * (SCALE * LOG2E))
        fac[t] = f
        l = l_s[t] * f
        w = w_s[t] * f
        return (
            l0 + jnp.where(low, l, zero),
            w0 + jnp.where(low, w, zero),
            l1 + jnp.where(low, zero, l),
            w1 + jnp.where(low, zero, w),
        )

    l0, w0, l1, w1 = lax.fori_loop(0, STEPS, sum_body, (zero, zero, zero, zero))
    inv = (1.0 / l0, 1.0 / l1)
    delta = (w0 / l0, w1 / l1)

    def second(t, s, j):
        low = s == 0
        f = (fac[t] * jnp.where(low, inv[0], inv[1]))[0:1, :]
        dl = jnp.where(low, delta[0], delta[1])[0:1, :]
        p = e_s[t] * f
        ds = (p * (d_s[t] - dl)).astype(jnp.bfloat16)
        pb = p.astype(jnp.bfloat16)
        rows = pl.ds(pl.multiple_of(j * BLOCK, BLOCK), BLOCK)
        keys = kv[rows, 0:HEAD]
        acc[rows, 0:HEAD] += jnp.dot(ds, q_n[s], preferred_element_type=jnp.float32)
        acc[rows, HEAD:2 * HEAD] += jnp.dot(pb, g_n[s], preferred_element_type=jnp.float32)
        dq_t[s] += lax.dot_general(
            keys, ds, (((0,), (0,)), ((), ())), preferred_element_type=jnp.float32
        )

    second(0, 0, n_low - 1)
    second(1, 1, n_high - 1)

    def second_body(t, carry):
        s, j = place(t)
        second(t + 2, s, j)
        return carry

    lax.fori_loop(0, STEPS - 2, second_body, 0)

    def cast_body(j, carry):
        rows = pl.ds(pl.multiple_of(j * BLOCK, BLOCK), BLOCK)
        stage[rows, 0:HEAD] = (acc[rows, 0:HEAD] * SCALE).astype(jnp.bfloat16)
        stage[rows, HEAD:2 * HEAD] = acc[rows, HEAD:2 * HEAD].astype(jnp.bfloat16)
        return carry

    lax.fori_loop(0, SEQ // BLOCK, cast_body, 0)
    copies = []
    for dc in range(NC):
        for dx in range(NX):
            for zd in range(NZ):
                who = (zd * NX + (x + dx) % NX) * NC + (c + dc) % NC
                p = pair[who]
                for half, span in ((0, p), (1, SPANS - 1 - p)):
                    n = ((dc * NX + dx) * NZ + zd) * 2 + half
                    copy = pltpu.make_async_copy(
                        stage.at[pl.ds(pl.multiple_of(span * SPAN, SPAN), SPAN), :],
                        out_ref.at[dc, dx, zd, pl.ds(half * SPAN, SPAN), :],
                        out_sem.at[n],
                    )
                    copy.start()
                    copies.append(copy)
    for s in range(2):
        dq = dq_t[s].T * SCALE
        for h in range(HEADS):
            dq_ref[pl.ds(s * SPAN, SPAN), pl.ds(h * HEAD, HEAD)] = dq[h * SPAN:(h + 1) * SPAN, :]
    for copy in copies:
        copy.wait()


def attention(meta, pair_order, queries, head_grads, chunks):
    smem = pl.BlockSpec(memory_space=pltpu.SMEM)
    vmem = pl.BlockSpec(memory_space=pltpu.VMEM)
    hbm = pl.BlockSpec(memory_space=pl.ANY)
    return pl.pallas_call(
        attention_kernel,
        out_shape=(
            jax.ShapeDtypeStruct((2 * SPAN, HEADS * HEAD), jnp.float32),
            jax.ShapeDtypeStruct((NC, NX, NZ, 2 * SPAN, 2 * HEAD), jnp.bfloat16),
        ),
        in_specs=[smem, smem, vmem, vmem] + [hbm] * 16,
        out_specs=(vmem, hbm),
        scratch_shapes=[
            pltpu.VMEM((SEQ, 2 * HEAD), jnp.bfloat16),
            pltpu.VMEM((STEPS, BLOCK, ROWS), jnp.float32),
            pltpu.VMEM((STEPS, BLOCK, ROWS), jnp.float32),
            pltpu.VMEM((SEQ, 2 * HEAD), jnp.float32),
            pltpu.VMEM((SEQ, 2 * HEAD), jnp.bfloat16),
            pltpu.VMEM((2, ROWS, HEAD), jnp.bfloat16),
            pltpu.VMEM((2, ROWS, HEAD), jnp.bfloat16),
            pltpu.VMEM((2, HEAD, ROWS), jnp.bfloat16),
            pltpu.VMEM((2, HEAD, ROWS), jnp.bfloat16),
            pltpu.VMEM((STEPS, 8, ROWS), jnp.float32),
            pltpu.VMEM((STEPS, 8, ROWS), jnp.float32),
            pltpu.VMEM((STEPS, 8, ROWS), jnp.float32),
            pltpu.VMEM((STEPS, 8, ROWS), jnp.float32),
            pltpu.VMEM((2, HEAD, ROWS), jnp.float32),
            pltpu.SemaphoreType.DMA((128,)),
            pltpu.SemaphoreType.DMA((128,)),
        ],
        compiler_params=pltpu.CompilerParams(vmem_limit_bytes=56 * 1024 * 1024),
        cost_estimate=pl.CostEstimate(flops=9 * 10**9, bytes_accessed=10**7, transcendentals=0),
        name="attention",
    )(meta, pair_order, queries, head_grads, *chunks)


def shift(value, axis, distance):
    size = lax.axis_size(axis)
    return lax.ppermute(value, axis, [(i, (i + distance) % size) for i in range(size)])


def wide(value):
    return value.astype(jnp.float32)


def shards(queries, keys, values, out_grad, out_weight, pair_order):
    y = lax.axis_index("y")
    meta = jnp.stack([lax.axis_index("z"), lax.axis_index("x"), lax.axis_index("c")])
    meta = meta.astype(jnp.int32)

    parts = [out_grad] + [shift(out_grad, "y", k) for k in (1, 2, 3)]
    whole = jnp.zeros((2 * SPAN, out_grad.shape[1] * NY), out_grad.dtype)
    for k, part in enumerate(parts):
        whole = lax.dynamic_update_slice(
            whole, part, (0, ((y + NY - k) % NY) * out_grad.shape[1])
        )
    head_grads = lax.dot_general(
        whole, out_weight, (((1,), (1,)), ((), ())), preferred_element_type=jnp.float32
    ).astype(jnp.bfloat16)

    own = jnp.concatenate([keys, values], axis=1)
    line = jnp.stack([own] + [shift(own, "x", k) for k in (1, 2, 3)])
    ahead, behind = line, line
    by_z = {0: line}
    for k in (1, 2, 3):
        ahead = shift(ahead, "z", 1)
        behind = shift(behind, "z", -1)
        by_z[k], by_z[NZ - k] = ahead, behind
    by_z[4] = jnp.concatenate([shift(ahead[:2], "z", 1), shift(behind[2:], "z", -1)])
    chunks = []
    for k in range(NZ):
        chunks += [by_z[k], shift(by_z[k], "c", 1)]

    query_gradient, terms = attention(meta, pair_order, queries, head_grads, chunks)

    other = shift(terms[1], "c", 1)
    terms = (wide(terms[0]) + wide(other)).astype(jnp.bfloat16)
    total = wide(terms[0])
    for k in (1, 2, 3):
        total = total + wide(shift(terms[k], "x", k))
    total = lax.all_to_all(total.astype(jnp.bfloat16), "z", 0, 0, tiled=True)
    total = jnp.sum(wide(total), axis=0)
    return query_gradient, total[:, :HEAD], total[:, HEAD:]


def solution(mesh):
    split = Mesh(mesh.devices.reshape(NZ, NX, NC, NY), ("z", "x", "c", "y"))
    ctx = ("z", "x", "c")
    return jax.shard_map(
        shards,
        mesh=split,
        in_specs=(P(ctx, "y"), P(ctx, "y"), P(ctx, "y"), P(ctx, "y"), P("y", None), P()),
        out_specs=(P(ctx, "y"), P(ctx, "y"), P(ctx, "y")),
        check_vma=False,
    )
```

time: 667 us -> 151 us (0.23)
  the two profiles are of different devices: /device:TPU:1 before, /device:TPU:16 now
where the time goes in v1:
time: 151 us
  waiting for transfers between devices  55.5 us (37%)
  Pallas kernels  29.3 us (19%)
  starting transfers between devices  29.1 us (19%)
  blocking collectives  20 us (13%)
  matrix products  7.64 us (5%)
  local copies, waits for them, and re-layouts  6.28 us (4%)
  other arithmetic  1.79 us (1%)
    ppermute x26, waiting for transfers between devices, shift(): lax.ppermute(value, axis, [(i, (i + distance) % size) for i in range(size)])  55.5 us
    pallas_call x1, Pallas kernels, attention(): pl.pallas_call(attention_kernel, out_shape=(jax.ShapeDtypeStruct((2 * SPA...  29.3 us
    ppermute x26, starting transfers between devices, shift(): lax.ppermute(value, axis, [(i, (i + distance) % size) for i in range(size)])  29.1 us
    all_to_all x1, blocking collectives, shards(): total = lax.all_to_all(total.astype(jnp.bfloat16), 'z', 0, 0, tiled=True)  20 us
    dot_general x1, matrix products, shards(): lax.dot_general(whole, out_weight, (((1,), (1,)), ((), ())), preferred_el...  7.64 us
  transfers between devices with their start and end apart: 26, of which 10 were waited for; matrix products, arithmetic and copies ran while one was open for 6% of the time, Pallas kernels for 0%

profile of v1, /device:TPU:16, one launch (start us, length us, event | category | flops | bytes accessed | tf_op | source)
XLA Modules:
  0.0 150.6 jit_solution(15527101341275700991)
XLA Ops:
  0.6 0.0 copy-start.1
  0.6 0.8 constant_dynamic-update-slice_fusion.1
  1.5 0.8 constant_dynamic-update-slice_fusion
  2.2 2.8 %collective-permute-start.5 = (bf16[128,256]{1,0:T(8,128)(2,1)S(1)}, bf16[128,256]{1,0:T(8,128)(2,1)S(1)}, u32[]{:S(2)}, u32[]{:S(2)}) collective-permute-start(bf16[128,256]{1,0:T(8,128)(2,1)S(1)} %constant_dynamic-update-slice_fusion), channel_id=1, source_target_pairs={{0,24},{8,0},{16,8},{24,16},{1,25},{9,1},{17,9},{25,17},{2,26},{10... | collective-permute-start | bytes 196616 | tf_op jit(solution)/shard_map/ppermute | solution.py:222
  5.1 0.8 collective-permute-start.4
  5.9 0.9 collective-permute-start.3
  6.7 0.5 collective-permute-done.5
  7.3 3.6 %collective-permute-done.4 = bf16[128,256]{1,0:T(8,128)(2,1)S(1)} collective-permute-done((bf16[128,256]{1,0:T(8,128)(2,1)S(1)}, bf16[128,256]{1,0:T(8,128)(2,1)S(1)}, u32[]{:S(2)}, u32[]{:S(2)}) %collective-permute-start.4) | collective-permute-done | bytes 65568 | tf_op jit(solution)/shard_map/ppermute | solution.py:222
  10.8 0.7 collective-permute-done.3
  11.6 5.9 %collective-permute-start.14 = (bf16[4,128,256]{2,1,0:T(8,128)(2,1)S(1)}, bf16[4,128,256]{2,1,0:T(8,128)(2,1)}, u32[]{:S(2)}, u32[]{:S(2)}) collective-permute-start(bf16[4,128,256]{2,1,0:T(8,128)(2,1)S(1)} %pad_maximum_fusion.refs_4_), channel_id=1, source_target_pairs={{0,224},{32,0},{64,32},{96,64},{128,96},{160,128},{192,160},{224,1... | collective-permute-start | bytes 786440 | tf_op jit(solution)/shard_map/ppermute | solution.py:222
  17.5 0.0 collective-permute-start.7
  17.5 1.3 collective-permute-start
  18.8 0.7 collective-permute-start.2
  19.5 1.5 %collective-permute-start.1 = (bf16[128,1536]{1,0:T(8,128)(2,1)}, bf16[128,1536]{1,0:T(8,128)(2,1)S(1)}, u32[]{:S(2)}, u32[]{:S(2)}) collective-permute-start(bf16[128,1536]{1,0:T(8,128)(2,1)} %param.9), channel_id=1, source_target_pairs={{0,2},{1,3},{2,0},{3,1},{4,6},{5,7},{6,4},{7,5},{8,10},{9,11},{10,... | collective-permute-start | bytes 1179656 | tf_op jit(solution)/shard_map/ppermute | solution.py:222
  21.1 0.6 collective-permute-done.14.refs_18_
  21.6 3.8 %collective-permute-start.15 = (bf16[4,128,256]{2,1,0:T(8,128)(2,1)}, bf16[4,128,256]{2,1,0:T(8,128)(2,1)}, u32[]{:S(2)}, u32[]{:S(2)}) collective-permute-start(bf16[4,128,256]{2,1,0:T(8,128)(2,1)} %collective-permute-done.14.refs_18_), channel_id=1, source_target_pairs={{0,224},{32,0},{64,32},{96,64},{128,96},{160,128},{192,160},{224,1... | collective-permute-start | bytes 786440 | tf_op jit(solution)/shard_map/ppermute | solution.py:222
  25.4 0.0 collective-permute-done.7.refs_6_
  25.4 0.0 collective-permute-start.9
  25.4 0.1 broadcast_in_dim.3
  25.7 0.6 pad_add_fusion.refs_0_
  26.3 9.0 %collective-permute-done = bf16[128,1536]{1,0:T(8,128)(2,1)S(1)} collective-permute-done((bf16[128,1536]{1,0:T(8,128)(2,1)}, bf16[128,1536]{1,0:T(8,128)(2,1)S(1)}, u32[]{:S(2)}, u32[]{:S(2)}) %collective-permute-start) | collective-permute-done | bytes 393248 | tf_op jit(solution)/shard_map/ppermute | solution.py:222
  35.3 0.0 collective-permute-start.6
  35.3 0.0 collective-permute-done.15.refs_16_
  35.3 3.0 %collective-permute-start.16 = (bf16[4,128,256]{2,1,0:T(8,128)(2,1)}, bf16[4,128,256]{2,1,0:T(8,128)(2,1)S(1)}, u32[]{:S(2)}, u32[]{:S(2)}) collective-permute-start(bf16[4,128,256]{2,1,0:T(8,128)(2,1)} %collective-permute-done.15.refs_16_), channel_id=1, source_target_pairs={{0,224},{32,0},{64,32},{96,64},{128,96},{160,128},{192,160},{224,1... | collective-permute-start | bytes 786440 | tf_op jit(solution)/shard_map/ppermute | solution.py:222
  38.3 0.0 collective-permute-done.9.refs_8_
  38.3 0.0 collective-permute-start.11
  38.3 0.0 collective-permute-done.1
  38.3 0.3 collective-permute-start.21
  38.7 6.1 %collective-permute-done.16.refs_14_ = bf16[4,128,256]{2,1,0:T(8,128)(2,1)S(1)} collective-permute-done((bf16[4,128,256]{2,1,0:T(8,128)(2,1)}, bf16[4,128,256]{2,1,0:T(8,128)(2,1)S(1)}, u32[]{:S(2)}, u32[]{:S(2)}) %collective-permute-start.16) | collective-permute-done | bytes 262176 | tf_op jit(solution)/shard_map/ppermute | solution.py:222
  44.8 0.0 collective-permute-start.8
  44.8 3.3 %collective-permute-done.11.refs_10_ = bf16[4,128,256]{2,1,0:T(8,128)(2,1)S(1)} collective-permute-done((bf16[4,128,256]{2,1,0:T(8,128)(2,1)}, bf16[4,128,256]{2,1,0:T(8,128)(2,1)S(1)}, u32[]{:S(2)}, u32[]{:S(2)}) %collective-permute-start.11) | collective-permute-done | bytes 262176 | tf_op jit(solution)/shard_map/ppermute | solution.py:222
  48.1 0.4 collective-permute-start.17
  48.5 0.0 collective-permute-done.2
  48.5 1.9 %collective-permute-start.13 = (bf16[2,128,256]{2,1,0:T(8,128)(2,1)S(1)}, bf16[2,128,256]{2,1,0:T(8,128)(2,1)S(1)}, u32[]{:S(2)}, u32[]{:S(2)}) collective-permute-start(bf16[2,128,256]{2,1,0:T(8,128)(2,1)S(1)} %slice.40), channel_id=1, source_target_pairs={{0,32},{32,64},{64,96},{96,128},{128,160},{160,192},{192,224},{224... | collective-permute-start | bytes 393224 | tf_op jit(solution)/shard_map/ppermute | solution.py:222
  50.5 5.2 %collective-permute-done.13 = bf16[2,128,256]{2,1,0:T(8,128)(2,1)S(1)} collective-permute-done((bf16[2,128,256]{2,1,0:T(8,128)(2,1)S(1)}, bf16[2,128,256]{2,1,0:T(8,128)(2,1)S(1)}, u32[]{:S(2)}, u32[]{:S(2)}) %collective-permute-start.13) | collective-permute-done | bytes 131104 | tf_op jit(solution)/shard_map/ppermute | solution.py:222
  55.7 0.6 collective-permute-start.10
  56.3 0.1 collective-permute-start.19
  56.4 0.5 collective-permute-start.12
  56.9 0.0 collective-permute-done.8.refs_7_
  56.9 0.1 collective-permute-start.18
  57.0 7.6 %convolution_convert_fusion.refs_3_ = bf16[128,768]{1,0:T(8,128)(2,1)} fusion(bf16[128,6144]{1,0:T(8,128)(2,1)S(1)} %constant_dynamic-update-slice_fusion.4, bf16[768,6144]{1,0:T(8,128)(2,1)} %param.10), kind=kOutput, calls=%fused_computation.3 | convolution fusion | flops 1208057856 | bytes 11206656 | tf_op jit(solution)/shard_map/dot_general | solution.py:240
  64.7 0.0 collective-permute-done.20.refs_17_
  64.7 0.0 collective-permute-done.10.refs_9_
  64.8 0.0 collective-permute-done.12.refs_11_
  64.8 0.0 collective-permute-done.18.refs_13_
  64.8 0.6 copy-done.9
  65.4 0.1 copy-done.10
  65.5 0.1 copy-done.11
  65.6 0.1 copy-done.12
  65.7 0.7 copy-done.13
  66.4 29.3 %attention.1 = (f32[128,768]{1,0:T(8,128)}, bf16[2,4,8,128,256]{4,3,2,1,0:T(8,128)(2,1)}) custom-call(s32[3]{0:T(128)} %pad_add_fusion.refs_0_, s32[64]{0:T(128)} %refs_1_.1, bf16[128,768]{1,0:T(8,128)(2,1)} %refs_2_.1, bf16[128,768]{1,0:T(8,128)(2,1)} %convolution_convert_fusion.refs_3_, bf16[4,128,256]{2,1,0:T(8,128)(2,1)} %copy-done.2, ...), custom_call_target="tpu_custom_call" | custom-call | flops 8999999488 | bytes 10000000 | tf_op jit(solution)/shard_map/attention/pallas_call | solution.py:188
  95.7 1.9 %slice_bitcast_fusion = bf16[4,8,128,256]{3,2,1,0:T(8,128)(2,1)S(1)} fusion(bf16[2,4,8,128,256]{4,3,2,1,0:T(8,128)(2,1)} %get-tuple-element.6), kind=kLoop, calls=%fused_computation.2 | loop fusion | bytes 4194304 | tf_op jit(solution)/shard_map/squeeze | solution.py:259
  97.6 0.5 collective-permute-start.22
  98.1 3.8 %collective-permute-done.22 = bf16[4,8,128,256]{3,2,1,0:T(8,128)(2,1)S(1)} collective-permute-done((bf16[4,8,128,256]{3,2,1,0:T(8,128)(2,1)S(1)}, bf16[4,8,128,256]{3,2,1,0:T(8,128)(2,1)S(1)}, u32[]{:S(2)}, u32[]{:S(2)}) %collective-permute-start.22) | collective-permute-done | bytes 2097184 | tf_op jit(solution)/shard_map/ppermute | solution.py:222
  101.9 0.8 fusion
  102.7 0.1 slice_bitcast_fusion.3
  102.9 0.1 collective-permute-start.23
  103.0 3.2 %collective-permute-start.25 = (bf16[8,128,256]{2,1,0:T(8,128)(2,1)S(1)}, bf16[8,128,256]{2,1,0:T(8,128)(2,1)S(1)}, u32[]{:S(2)}, u32[]{:S(2)}) collective-permute-start(bf16[8,128,256]{2,1,0:T(8,128)(2,1)S(1)} %get-tuple-element.8), channel_id=1, source_target_pairs={{0,24},{8,0},{16,8},{24,16},{1,25},{9,1},{17,9},{25,17},{2,26},{10... | collective-permute-start | bytes 1572872 | tf_op jit(solution)/shard_map/ppermute | solution.py:222
  106.2 0.6 collective-permute-start.24
  106.8 22.8 %collective-permute-done.23 = bf16[8,128,256]{2,1,0:T(8,128)(2,1)S(1)} collective-permute-done((bf16[8,128,256]{2,1,0:T(8,128)(2,1)S(1)}, bf16[8,128,256]{2,1,0:T(8,128)(2,1)S(1)}, u32[]{:S(2)}, u32[]{:S(2)}) %collective-permute-start.23) | collective-permute-done | bytes 524320 | tf_op jit(solution)/shard_map/ppermute | solution.py:222
  129.6 0.3 fusion.3
  129.9 20.0 %all_to_all.5 = bf16[8,128,256]{2,1,0:T(8,128)(2,1)S(1)} all-to-all(bf16[8,128,256]{2,1,0:T(8,128)(2,1)S(1)} %fusion.3), channel_id=1, replica_groups=mesh['z'=8,'x'=4,'c'=2,'y'=4] {'z'}, dimensions={0} | all-to-all | bytes 1048576 | tf_op jit(solution)/shard_map/all_to_all | solution.py:264
  149.9 0.1 convert_reduce_fusion
  149.9 0.7 fusion.4
  (38 shorter events, 0.3 us)
Async XLA Ops:
  0.6 25.0 %copy-start.1 = (bf16[128,1536]{1,0:T(8,128)(2,1)S(1)}, bf16[128,1536]{1,0:T(8,128)(2,1)}, u32[]{:S(2)}) copy-start(bf16[128,1536]{1,0:T(8,128)(2,1)} %param.9) | copy-start | bytes 1179652
  2.2 5.1 %collective-permute-start.5 = (bf16[128,256]{1,0:T(8,128)(2,1)S(1)}, bf16[128,256]{1,0:T(8,128)(2,1)S(1)}, u32[]{:S(2)}, u32[]{:S(2)}) collective-permute-start(bf16[128,256]{1,0:T(8,128)(2,1)S(1)} %constant_dynamic-update-slice_fusion), channel_id=1, source_target_pairs={{0,24},{8,0},{16,8},{24,16},{1,25},{9,1},{17,9},{25,17},{2,26},{10... | collective-permute-start | bytes 196616 | tf_op jit(solution)/shard_map/ppermute | solution.py:222
  5.1 5.8 %collective-permute-start.4 = (bf16[128,256]{1,0:T(8,128)(2,1)S(1)}, bf16[128,256]{1,0:T(8,128)(2,1)S(1)}, u32[]{:S(2)}, u32[]{:S(2)}) collective-permute-start(bf16[128,256]{1,0:T(8,128)(2,1)S(1)} %constant_dynamic-update-slice_fusion), channel_id=1, source_target_pairs={{0,16},{8,24},{16,0},{24,8},{1,17},{9,25},{17,1},{25,9},{2,18},{10... | collective-permute-start | bytes 196616 | tf_op jit(solution)/shard_map/ppermute | solution.py:222
  5.9 5.7 %collective-permute-start.3 = (bf16[128,256]{1,0:T(8,128)(2,1)S(1)}, bf16[128,256]{1,0:T(8,128)(2,1)S(1)}, u32[]{:S(2)}, u32[]{:S(2)}) collective-permute-start(bf16[128,256]{1,0:T(8,128)(2,1)S(1)} %constant_dynamic-update-slice_fusion), channel_id=1, source_target_pairs={{0,8},{8,16},{16,24},{24,0},{1,9},{9,17},{17,25},{25,1},{2,10},{10... | collective-permute-start | bytes 196616 | tf_op jit(solution)/shard_map/ppermute | solution.py:222
  11.6 33.3 %copy-start.2 = (bf16[4,128,256]{2,1,0:T(8,128)(2,1)}, bf16[4,128,256]{2,1,0:T(8,128)(2,1)S(1)}, u32[]{:S(2)}) copy-start(bf16[4,128,256]{2,1,0:T(8,128)(2,1)S(1)} %pad_maximum_fusion.refs_4_) | copy-start | bytes 786436
  11.6 10.1 %collective-permute-start.14 = (bf16[4,128,256]{2,1,0:T(8,128)(2,1)S(1)}, bf16[4,128,256]{2,1,0:T(8,128)(2,1)}, u32[]{:S(2)}, u32[]{:S(2)}) collective-permute-start(bf16[4,128,256]{2,1,0:T(8,128)(2,1)S(1)} %pad_maximum_fusion.refs_4_), channel_id=1, source_target_pairs={{0,224},{32,0},{64,32},{96,64},{128,96},{160,128},{192,160},{224,1... | collective-permute-start | bytes 786440 | tf_op jit(solution)/shard_map/ppermute | solution.py:222
  17.5 7.9 %collective-permute-start.7 = (bf16[4,128,256]{2,1,0:T(8,128)(2,1)S(1)}, bf16[4,128,256]{2,1,0:T(8,128)(2,1)}, u32[]{:S(2)}, u32[]{:S(2)}) collective-permute-start(bf16[4,128,256]{2,1,0:T(8,128)(2,1)S(1)} %pad_maximum_fusion.refs_4_), channel_id=1, source_target_pairs={{0,32},{32,64},{64,96},{96,128},{128,160},{160,192},{192,224},{224... | collective-permute-start | bytes 786440 | tf_op jit(solution)/shard_map/ppermute | solution.py:222
  17.5 17.8 %collective-permute-start = (bf16[128,1536]{1,0:T(8,128)(2,1)}, bf16[128,1536]{1,0:T(8,128)(2,1)S(1)}, u32[]{:S(2)}, u32[]{:S(2)}) collective-permute-start(bf16[128,1536]{1,0:T(8,128)(2,1)} %param.9), channel_id=1, source_target_pairs={{0,1},{1,2},{2,3},{3,0},{4,5},{5,6},{6,7},{7,4},{8,9},{9,10},{10,1... | collective-permute-start | bytes 1179656 | tf_op jit(solution)/shard_map/ppermute | solution.py:222
  18.8 29.7 %collective-permute-start.2 = (bf16[128,1536]{1,0:T(8,128)(2,1)}, bf16[128,1536]{1,0:T(8,128)(2,1)S(1)}, u32[]{:S(2)}, u32[]{:S(2)}) collective-permute-start(bf16[128,1536]{1,0:T(8,128)(2,1)} %param.9), channel_id=1, source_target_pairs={{0,3},{1,0},{2,1},{3,2},{4,7},{5,4},{6,5},{7,6},{8,11},{9,8},{10,9... | collective-permute-start | bytes 1179656 | tf_op jit(solution)/shard_map/ppermute | solution.py:222
  19.5 18.8 %collective-permute-start.1 = (bf16[128,1536]{1,0:T(8,128)(2,1)}, bf16[128,1536]{1,0:T(8,128)(2,1)S(1)}, u32[]{:S(2)}, u32[]{:S(2)}) collective-permute-start(bf16[128,1536]{1,0:T(8,128)(2,1)} %param.9), channel_id=1, source_target_pairs={{0,2},{1,3},{2,0},{3,1},{4,6},{5,7},{6,4},{7,5},{8,10},{9,11},{10,... | collective-permute-start | bytes 1179656 | tf_op jit(solution)/shard_map/ppermute | solution.py:222
  21.6 13.7 %collective-permute-start.15 = (bf16[4,128,256]{2,1,0:T(8,128)(2,1)}, bf16[4,128,256]{2,1,0:T(8,128)(2,1)}, u32[]{:S(2)}, u32[]{:S(2)}) collective-permute-start(bf16[4,128,256]{2,1,0:T(8,128)(2,1)} %collective-permute-done.14.refs_18_), channel_id=1, source_target_pairs={{0,224},{32,0},{64,32},{96,64},{128,96},{160,128},{192,160},{224,1... | collective-permute-start | bytes 786440 | tf_op jit(solution)/shard_map/ppermute | solution.py:222
  25.4 12.8 %collective-permute-start.9 = (bf16[4,128,256]{2,1,0:T(8,128)(2,1)}, bf16[4,128,256]{2,1,0:T(8,128)(2,1)}, u32[]{:S(2)}, u32[]{:S(2)}) collective-permute-start(bf16[4,128,256]{2,1,0:T(8,128)(2,1)} %collective-permute-done.7.refs_6_), channel_id=1, source_target_pairs={{0,32},{32,64},{64,96},{96,128},{128,160},{160,192},{192,224},{224... | collective-permute-start | bytes 786440 | tf_op jit(solution)/shard_map/ppermute | solution.py:222
  35.3 21.0 %collective-permute-start.6 = (bf16[4,128,256]{2,1,0:T(8,128)(2,1)S(1)}, bf16[4,128,256]{2,1,0:T(8,128)(2,1)S(1)}, u32[]{:S(2)}, u32[]{:S(2)}) collective-permute-start(bf16[4,128,256]{2,1,0:T(8,128)(2,1)S(1)} %pad_maximum_fusion.refs_4_), channel_id=1, source_target_pairs={{0,4},{4,0},{1,5},{5,1},{2,6},{6,2},{3,7},{7,3},{8,12},{12,8},{9,1... | collective-permute-start | bytes 786440 | tf_op jit(solution)/shard_map/ppermute | solution.py:222
  35.3 9.5 %collective-permute-start.16 = (bf16[4,128,256]{2,1,0:T(8,128)(2,1)}, bf16[4,128,256]{2,1,0:T(8,128)(2,1)S(1)}, u32[]{:S(2)}, u32[]{:S(2)}) collective-permute-start(bf16[4,128,256]{2,1,0:T(8,128)(2,1)} %collective-permute-done.15.refs_16_), channel_id=1, source_target_pairs={{0,224},{32,0},{64,32},{96,64},{128,96},{160,128},{192,160},{224,1... | collective-permute-start | bytes 786440 | tf_op jit(solution)/shard_map/ppermute | solution.py:222
  38.3 9.9 %collective-permute-start.11 = (bf16[4,128,256]{2,1,0:T(8,128)(2,1)}, bf16[4,128,256]{2,1,0:T(8,128)(2,1)S(1)}, u32[]{:S(2)}, u32[]{:S(2)}) collective-permute-start(bf16[4,128,256]{2,1,0:T(8,128)(2,1)} %collective-permute-done.9.refs_8_), channel_id=1, source_target_pairs={{0,32},{32,64},{64,96},{96,128},{128,160},{160,192},{192,224},{224... | collective-permute-start | bytes 786440 | tf_op jit(solution)/shard_map/ppermute | solution.py:222
  38.3 18.1 %collective-permute-start.21 = (bf16[4,128,256]{2,1,0:T(8,128)(2,1)}, bf16[4,128,256]{2,1,0:T(8,128)(2,1)S(1)}, u32[]{:S(2)}, u32[]{:S(2)}) collective-permute-start(bf16[4,128,256]{2,1,0:T(8,128)(2,1)} %collective-permute-done.14.refs_18_), channel_id=1, source_target_pairs={{0,4},{4,0},{1,5},{5,1},{2,6},{6,2},{3,7},{7,3},{8,12},{12,8},{9,1... | collective-permute-start | bytes 786440 | tf_op jit(solution)/shard_map/ppermute | solution.py:222
  44.8 19.9 %copy-start.3 = (bf16[4,128,256]{2,1,0:T(8,128)(2,1)}, bf16[4,128,256]{2,1,0:T(8,128)(2,1)S(1)}, u32[]{:S(2)}) copy-start(bf16[4,128,256]{2,1,0:T(8,128)(2,1)S(1)} %collective-permute-done.16.refs_14_) | copy-start | bytes 786436
  44.8 12.1 %collective-permute-start.8 = (bf16[4,128,256]{2,1,0:T(8,128)(2,1)}, bf16[4,128,256]{2,1,0:T(8,128)(2,1)S(1)}, u32[]{:S(2)}, u32[]{:S(2)}) collective-permute-start(bf16[4,128,256]{2,1,0:T(8,128)(2,1)} %collective-permute-done.7.refs_6_), channel_id=1, source_target_pairs={{0,4},{4,0},{1,5},{5,1},{2,6},{6,2},{3,7},{7,3},{8,12},{12,8},{9,1... | collective-permute-start | bytes 786440 | tf_op jit(solution)/shard_map/ppermute | solution.py:222
  48.1 16.6 %copy-start.4 = (bf16[4,128,256]{2,1,0:T(8,128)(2,1)}, bf16[4,128,256]{2,1,0:T(8,128)(2,1)S(1)}, u32[]{:S(2)}) copy-start(bf16[4,128,256]{2,1,0:T(8,128)(2,1)S(1)} %collective-permute-done.11.refs_10_) | copy-start | bytes 786436
  48.1 7.5 %collective-permute-start.17 = (bf16[2,128,256]{2,1,0:T(8,128)(2,1)S(1)}, bf16[2,128,256]{2,1,0:T(8,128)(2,1)S(1)}, u32[]{:S(2)}, u32[]{:S(2)}) collective-permute-start(bf16[2,128,256]{2,1,0:T(8,128)(2,1)S(1)} %slice.41), channel_id=1, source_target_pairs={{0,224},{32,0},{64,32},{96,64},{128,96},{160,128},{192,160},{224,1... | collective-permute-start | bytes 393224 | tf_op jit(solution)/shard_map/ppermute | solution.py:222
  48.5 7.1 %collective-permute-start.13 = (bf16[2,128,256]{2,1,0:T(8,128)(2,1)S(1)}, bf16[2,128,256]{2,1,0:T(8,128)(2,1)S(1)}, u32[]{:S(2)}, u32[]{:S(2)}) collective-permute-start(bf16[2,128,256]{2,1,0:T(8,128)(2,1)S(1)} %slice.40), channel_id=1, source_target_pairs={{0,32},{32,64},{64,96},{96,128},{128,160},{160,192},{192,224},{224... | collective-permute-start | bytes 393224 | tf_op jit(solution)/shard_map/ppermute | solution.py:222
  55.6 9.1 %collective-permute-start.20 = (bf16[4,128,256]{2,1,0:T(8,128)(2,1)}, bf16[4,128,256]{2,1,0:T(8,128)(2,1)S(1)}, u32[]{:S(2)}, u32[]{:S(2)}) collective-permute-start(bf16[4,128,256]{2,1,0:T(8,128)(2,1)} %collective-permute-done.15.refs_16_), channel_id=1, source_target_pairs={{0,4},{4,0},{1,5},{5,1},{2,6},{6,2},{3,7},{7,3},{8,12},{12,8},{9,1... | collective-permute-start | bytes 786440 | tf_op jit(solution)/shard_map/ppermute | solution.py:222
  55.7 9.1 %collective-permute-start.10 = (bf16[4,128,256]{2,1,0:T(8,128)(2,1)}, bf16[4,128,256]{2,1,0:T(8,128)(2,1)S(1)}, u32[]{:S(2)}, u32[]{:S(2)}) collective-permute-start(bf16[4,128,256]{2,1,0:T(8,128)(2,1)} %collective-permute-done.9.refs_8_), channel_id=1, source_target_pairs={{0,4},{4,0},{1,5},{5,1},{2,6},{6,2},{3,7},{7,3},{8,12},{12,8},{9,1... | collective-permute-start | bytes 786440 | tf_op jit(solution)/shard_map/ppermute | solution.py:222
  56.3 8.4 %copy-start.5 = (bf16[4,128,256]{2,1,0:T(8,128)(2,1)}, bf16[4,128,256]{2,1,0:T(8,128)(2,1)S(1)}, u32[]{:S(2)}) copy-start(bf16[4,128,256]{2,1,0:T(8,128)(2,1)S(1)} %constant_dynamic-update-slice_fusion.2.refs_12_) | copy-start | bytes 786436
  56.3 8.4 %copy-start.6 = (bf16[4,128,256]{2,1,0:T(8,128)(2,1)}, bf16[4,128,256]{2,1,0:T(8,128)(2,1)S(1)}, u32[]{:S(2)}) copy-start(bf16[4,128,256]{2,1,0:T(8,128)(2,1)S(1)} %collective-permute-done.6.refs_5_) | copy-start | bytes 786436
  56.3 8.4 %collective-permute-start.19 = (bf16[4,128,256]{2,1,0:T(8,128)(2,1)S(1)}, bf16[4,128,256]{2,1,0:T(8,128)(2,1)S(1)}, u32[]{:S(2)}, u32[]{:S(2)}) collective-permute-start(bf16[4,128,256]{2,1,0:T(8,128)(2,1)S(1)} %collective-permute-done.16.refs_14_), channel_id=1, source_target_pairs={{0,4},{4,0},{1,5},{5,1},{2,6},{6,2},{3,7},{7,3},{8,12},{12,8},{9,1... | collective-permute-start | bytes 786440 | tf_op jit(solution)/shard_map/ppermute | solution.py:222
  56.4 8.3 %copy-start.7 = (bf16[4,128,256]{2,1,0:T(8,128)(2,1)}, bf16[4,128,256]{2,1,0:T(8,128)(2,1)S(1)}, u32[]{:S(2)}) copy-start(bf16[4,128,256]{2,1,0:T(8,128)(2,1)S(1)} %collective-permute-done.21.refs_19_) | copy-start | bytes 786436
  56.4 8.3 %collective-permute-start.12 = (bf16[4,128,256]{2,1,0:T(8,128)(2,1)S(1)}, bf16[4,128,256]{2,1,0:T(8,128)(2,1)S(1)}, u32[]{:S(2)}, u32[]{:S(2)}) collective-permute-start(bf16[4,128,256]{2,1,0:T(8,128)(2,1)S(1)} %collective-permute-done.11.refs_10_), channel_id=1, source_target_pairs={{0,4},{4,0},{1,5},{5,1},{2,6},{6,2},{3,7},{7,3},{8,12},{12,8},{9,1... | collective-permute-start | bytes 786440 | tf_op jit(solution)/shard_map/ppermute | solution.py:222
  56.9 7.8 %copy-start.8 = (bf16[4,128,256]{2,1,0:T(8,128)(2,1)}, bf16[4,128,256]{2,1,0:T(8,128)(2,1)S(1)}, u32[]{:S(2)}) copy-start(bf16[4,128,256]{2,1,0:T(8,128)(2,1)S(1)} %collective-permute-done.8.refs_7_) | copy-start | bytes 786436
  56.9 7.9 %collective-permute-start.18 = (bf16[4,128,256]{2,1,0:T(8,128)(2,1)S(1)}, bf16[4,128,256]{2,1,0:T(8,128)(2,1)S(1)}, u32[]{:S(2)}, u32[]{:S(2)}) collective-permute-start(bf16[4,128,256]{2,1,0:T(8,128)(2,1)S(1)} %constant_dynamic-update-slice_fusion.2.refs_12_), channel_id=1, source_target_pairs={{0,4},{4,0},{1,5},{5,1},{2,6},{6,2},{3,7},{7,3},{8,12},{12,8},{9,1... | collective-permute-start | bytes 786440 | tf_op jit(solution)/shard_map/ppermute | solution.py:222
  64.7 0.7 copy-start.9
  64.7 0.8 copy-start.10
  64.8 0.9 copy-start.11
  64.8 1.0 copy-start.12
  65.7 0.7 copy-start.13
  95.7 6.2 %copy-start = (bf16[2,4,8,128,256]{4,3,2,1,0:T(8,128)(2,1)S(1)}, bf16[2,4,8,128,256]{4,3,2,1,0:T(8,128)(2,1)}, u32[]{:S(2)}) copy-start(bf16[2,4,8,128,256]{4,3,2,1,0:T(8,128)(2,1)} %get-tuple-element.6) | copy-start | bytes 12582916
  97.6 4.3 %collective-permute-start.22 = (bf16[4,8,128,256]{3,2,1,0:T(8,128)(2,1)S(1)}, bf16[4,8,128,256]{3,2,1,0:T(8,128)(2,1)S(1)}, u32[]{:S(2)}, u32[]{:S(2)}) collective-permute-start(bf16[4,8,128,256]{3,2,1,0:T(8,128)(2,1)S(1)} %slice_bitcast_fusion), channel_id=1, source_target_pairs={{0,4},{4,0},{1,5},{5,1},{2,6},{6,2},{3,7},{7,3},{8,12},{12,8},{9,1... | collective-permute-start | bytes 6291464 | tf_op jit(solution)/shard_map/ppermute | solution.py:222
  102.9 26.7 %collective-permute-start.23 = (bf16[8,128,256]{2,1,0:T(8,128)(2,1)S(1)}, bf16[8,128,256]{2,1,0:T(8,128)(2,1)S(1)}, u32[]{:S(2)}, u32[]{:S(2)}) collective-permute-start(bf16[8,128,256]{2,1,0:T(8,128)(2,1)S(1)} %get-tuple-element.7), channel_id=1, source_target_pairs={{0,8},{8,16},{16,24},{24,0},{1,9},{9,17},{17,25},{25,1},{2,10},{10... | collective-permute-start | bytes 1572872 | tf_op jit(solution)/shard_map/ppermute | solution.py:222
  103.0 26.6 %collective-permute-start.25 = (bf16[8,128,256]{2,1,0:T(8,128)(2,1)S(1)}, bf16[8,128,256]{2,1,0:T(8,128)(2,1)S(1)}, u32[]{:S(2)}, u32[]{:S(2)}) collective-permute-start(bf16[8,128,256]{2,1,0:T(8,128)(2,1)S(1)} %get-tuple-element.8), channel_id=1, source_target_pairs={{0,24},{8,0},{16,8},{24,16},{1,25},{9,1},{17,9},{25,17},{2,26},{10... | collective-permute-start | bytes 1572872 | tf_op jit(solution)/shard_map/ppermute | solution.py:222
  106.2 23.4 %collective-permute-start.24 = (bf16[8,128,256]{2,1,0:T(8,128)(2,1)S(1)}, bf16[8,128,256]{2,1,0:T(8,128)(2,1)S(1)}, u32[]{:S(2)}, u32[]{:S(2)}) collective-permute-start(bf16[8,128,256]{2,1,0:T(8,128)(2,1)S(1)} %get-tuple-element.9), channel_id=1, source_target_pairs={{0,16},{8,24},{16,0},{24,8},{1,17},{9,25},{17,1},{25,9},{2,18},{10... | collective-permute-start | bytes 1572872 | tf_op jit(solution)/shard_map/ppermute | solution.py:222

commit v2 on v0

v2 whole, which is shorter than its diff:
```python
import jax
import jax.numpy as jnp
from jax import lax
from jax.experimental import pallas as pl
from jax.experimental.pallas import tpu as pltpu
from jax.sharding import Mesh, PartitionSpec as P

HEAD = 128
HEADS = 6
SPAN = 64
SPANS = 128
ROWS = HEADS * SPAN
BLOCK = 256
PER_BLOCK = BLOCK // SPAN
LOG2E = 1.4426950408889634
SCALE = HEAD ** -0.5
NZ, NX, NC, NY = 8, 4, 2, 4
QSETS = 2 * NX
KEY_DEVICES = NZ * NC
KEY_SPANS = 2 * KEY_DEVICES
KEYS = KEY_SPANS * SPAN
MAX_STEPS = 48
T_RANK, T_SPAN, T_QSPAN, T_QSET, T_BLOCK, T_COUNT, T_X, T_C = (
    0, 16, 48, 64, 112, 160, 161, 162
)
TABLE = 192
SPREAD_FLOPS = 2 * 10**10
LOW = -1e30
PAIR_STEPS = 2


def table_kernel(pair, table):
    z, x, c = lax.axis_index("z"), lax.axis_index("x"), lax.axis_index("c")
    keys = [pair[((i // NC) * NX + x) * NC + i % NC] for i in range(KEY_DEVICES)]
    ranks = [jnp.int32(0)] * KEY_DEVICES
    for i in range(KEY_DEVICES):
        for j in range(i):
            less = (keys[j] < keys[i]).astype(jnp.int32)
            ranks[i] = ranks[i] + less
            ranks[j] = ranks[j] + (1 - less)
    for i in range(KEY_DEVICES):
        table[T_RANK + i] = ranks[i]
        table[T_SPAN + ranks[i]] = keys[i]
        table[T_SPAN + KEY_SPANS - 1 - ranks[i]] = SPANS - 1 - keys[i]
    table[T_X] = x
    table[T_C] = c
    end = jnp.int32(0)
    for u in range(QSETS):
        low = pair[(z * NX + u // 2) * NC + c]
        below = jnp.int32(0)
        same = jnp.int32(0)
        for key in keys:
            below = below + (key < low).astype(jnp.int32)
            same = same + (key == low).astype(jnp.int32)
        if u % 2 == 0:
            table[T_QSPAN + u] = low
            seen = below + same
        else:
            table[T_QSPAN + u] = SPANS - 1 - low
            seen = KEY_SPANS - below
        count = (seen + PER_BLOCK - 1) // PER_BLOCK

        def fill(j, carry, u=u, end=end):
            table[T_QSET + end + j] = u
            table[T_BLOCK + end + j] = j
            return carry

        lax.fori_loop(0, count, fill, 0)
        end = end + count
    table[T_COUNT] = end
    table[T_QSPAN + QSETS] = -SPANS
    table[T_QSET + end] = QSETS
    table[T_BLOCK + end] = 0


def tables(pair_order):
    return pl.pallas_call(
        table_kernel,
        out_shape=jax.ShapeDtypeStruct((TABLE,), jnp.int32),
        in_specs=[SMEM],
        out_specs=SMEM,
        cost_estimate=pl.CostEstimate(flops=10**6, bytes_accessed=10**3, transcendentals=0),
        name="tables",
    )(pair_order)


def masked_scores(table, keys, q_t, u, j):
    sc = jnp.dot(keys, q_t[u], preferred_element_type=jnp.float32)
    row = lax.broadcasted_iota(jnp.int32, (SPAN, ROWS), 0)
    col = lax.broadcasted_iota(jnp.int32, (SPAN, ROWS), 1) % SPAN
    ahead = row - col
    q_span = table[T_QSPAN + u]
    pieces = []
    for i in range(PER_BLOCK):
        room = (q_span - table[T_SPAN + j * PER_BLOCK + i]) * SPAN
        pieces.append(jnp.where(ahead <= room, sc[i * SPAN:(i + 1) * SPAN, :], -jnp.inf))
    return jnp.concatenate(pieces, axis=0)


def block_rows(j):
    return pl.ds(pl.multiple_of(j * BLOCK, BLOCK), BLOCK)


def forward_kernel(table, *refs):
    queries = refs[:NX]
    own, other, kv, q_n, q_t, stats, o_t, m_s = refs[NX:]
    x = table[T_X]
    for i in range(KEY_DEVICES):
        dc, z = i // NZ, i % NZ
        chunk = (own, other)[dc]
        rank = table[T_RANK + z * NC + (table[T_C] + dc) % NC]
        for half, slot in ((0, rank), (1, KEY_SPANS - 1 - rank)):
            kv[pl.ds(pl.multiple_of(slot * SPAN, SPAN), SPAN), :] = (
                chunk[z, pl.ds(half * SPAN, SPAN), :]
            )
    for dx in range(NX):
        base = ((x + NX - dx) % NX) * 2
        for s in range(2):
            for h in range(HEADS):
                q_n[base + s, pl.ds(h * SPAN, SPAN), :] = (
                    queries[dx][pl.ds(s * SPAN, SPAN), pl.ds(h * HEAD, HEAD)]
                )
            q_t[base + s] = q_n[base + s].T
    q_t[QSETS] = jnp.zeros((HEAD, ROWS), jnp.bfloat16)
    o_t[...] = jnp.zeros_like(o_t)
    stats[1] = jnp.zeros((QSETS + 1, 8, ROWS), jnp.float32)
    m_s[...] = jnp.full_like(m_s, LOW)

    def body(i, carry):
        us = [table[T_QSET + i * PAIR_STEPS + k] for k in range(PAIR_STEPS)]
        js = [table[T_BLOCK + i * PAIR_STEPS + k] for k in range(PAIR_STEPS)]
        scs = [masked_scores(table, kv[block_rows(j), 0:HEAD], q_t, u, j) for u, j in zip(us, js)]
        tops = [jnp.max(sc, axis=0, keepdims=True) for sc in scs]
        for u, j, sc, top in zip(us, js, scs, tops):
            old = m_s[u]
            new = jnp.maximum(old, top)
            f = jnp.exp2((old - new) * (SCALE * LOG2E))
            e = jnp.exp2((sc - new[0:1, :]) * (SCALE * LOG2E))
            m_s[u] = new
            stats[1, u] = stats[1, u] * f + jnp.sum(e, axis=0, keepdims=True)
            o_t[u] = o_t[u] * f[0:1, :] + lax.dot_general(
                kv[block_rows(j), HEAD:2 * HEAD], e.astype(jnp.bfloat16),
                (((0,), (0,)), ((), ())), preferred_element_type=jnp.float32,
            )
        return carry

    lax.fori_loop(0, (table[T_COUNT] + PAIR_STEPS - 1) // PAIR_STEPS, body, 0)
    stats[0] = m_s[...]


def weight_kernel(table, *refs):
    grads = refs[:NX]
    stats, o_t = refs[NX:NX + 2]
    g_n, g_t, stats_out = refs[NX + 2:]
    x = table[T_X]
    for dx in range(NX):
        base = ((x + NX - dx) % NX) * 2
        for s in range(2):
            u = base + s
            for h in range(HEADS):
                g_n[u, pl.ds(h * SPAN, SPAN), :] = (
                    grads[dx][pl.ds(s * SPAN, SPAN), pl.ds(h * HEAD, HEAD)]
                )
            turned = g_n[u].T
            g_t[u] = turned
            w = jnp.sum(turned.astype(jnp.float32) * o_t[u], axis=0, keepdims=True)
            stats_out[2, pl.ds(u, 1), :] = w
            stats_out[0, pl.ds(u, 1), :] = stats[0, u, 0:1, :]
            stats_out[1, pl.ds(u, 1), :] = stats[1, u, 0:1, :]
    g_n[QSETS] = jnp.zeros((ROWS, HEAD), jnp.bfloat16)
    g_t[QSETS] = jnp.zeros((HEAD, ROWS), jnp.bfloat16)


def backward_kernel(table, *refs):
    stats = refs[:NX]
    kv, q_n, q_t, g_n, g_t, own_ref, part_ref, out_ref = refs[NX:NX + 8]
    acc, dq_t, lse_s, delta_s = refs[NX + 8:]
    x = table[T_X]
    top = stats[0][0]
    for r in stats[1:]:
        top = jnp.maximum(top, r[0])
    total = jnp.zeros((QSETS, ROWS), jnp.float32)
    weight = jnp.zeros((QSETS, ROWS), jnp.float32)
    for r in stats:
        f = jnp.exp2((r[0] - top) * (SCALE * LOG2E))
        total = total + r[1] * f
        weight = weight + r[2] * f
    lse = top * (SCALE * LOG2E) + jnp.log2(total)
    delta = weight / total
    for u in range(QSETS):
        lse_s[u] = jnp.broadcast_to(lse[u:u + 1, :], (8, ROWS))
        delta_s[u] = jnp.broadcast_to(delta[u:u + 1, :], (8, ROWS))
    lse_s[QSETS] = jnp.zeros((8, ROWS), jnp.float32)
    delta_s[QSETS] = jnp.zeros((8, ROWS), jnp.float32)
    acc[...] = jnp.zeros_like(acc)
    dq_t[...] = jnp.zeros_like(dq_t)

    def body(i, carry):
        us = [table[T_QSET + i * PAIR_STEPS + k] for k in range(PAIR_STEPS)]
        js = [table[T_BLOCK + i * PAIR_STEPS + k] for k in range(PAIR_STEPS)]
        scs = [masked_scores(table, kv[block_rows(j), 0:HEAD], q_t, u, j) for u, j in zip(us, js)]
        dps = [
            jnp.dot(kv[block_rows(j), HEAD:2 * HEAD], g_t[u], preferred_element_type=jnp.float32)
            for u, j in zip(us, js)
        ]
        for u, j, sc, dp in zip(us, js, scs, dps):
            p = jnp.exp2(sc * (SCALE * LOG2E) - lse_s[u][0:1, :])
            ds = (p * (dp - delta_s[u][0:1, :])).astype(jnp.bfloat16)
            rows = block_rows(j)
            acc[rows, HEAD:2 * HEAD] += jnp.dot(
                p.astype(jnp.bfloat16), g_n[u], preferred_element_type=jnp.float32
            )
            acc[rows, 0:HEAD] += jnp.dot(ds, q_n[u], preferred_element_type=jnp.float32)
            dq_t[u] += lax.dot_general(
                kv[rows, 0:HEAD], ds, (((0,), (0,)), ((), ())), preferred_element_type=jnp.float32
            )
        return carry

    lax.fori_loop(0, (table[T_COUNT] + PAIR_STEPS - 1) // PAIR_STEPS, body, 0)

    for i in range(KEY_DEVICES):
        rank = table[T_RANK + i]
        place = ((i + table[T_C]) % NC) * NZ + i // NC
        for half, slot in ((0, rank), (1, KEY_SPANS - 1 - rank)):
            rows = pl.ds(pl.multiple_of(slot * SPAN, SPAN), SPAN)
            out_ref[place, pl.ds(half * SPAN, SPAN), 0:HEAD] = (acc[rows, 0:HEAD] * SCALE).astype(jnp.bfloat16)
            out_ref[place, pl.ds(half * SPAN, SPAN), HEAD:2 * HEAD] = (
                acc[rows, HEAD:2 * HEAD].astype(jnp.bfloat16)
            )
    for dx in range(NX):
        base = ((x + dx) % NX) * 2
        for s in range(2):
            dq = dq_t[base + s].T * SCALE
            for h in range(HEADS):
                piece = dq[h * SPAN:(h + 1) * SPAN, :]
                rows, cols = pl.ds(s * SPAN, SPAN), pl.ds(h * HEAD, HEAD)
                if dx == 0:
                    own_ref[rows, cols] = piece
                else:
                    part_ref[dx - 1, rows, cols] = piece.astype(jnp.bfloat16)


def part_columns(k, columns):
    owner = (lax.axis_index("y") + NY - k) % NY
    return pl.ds(pl.multiple_of(owner * columns, columns), columns)


def weight_product(weight, part):
    return lax.dot_general(
        weight, part[...], (((1,), (1,)), ((), ())), preferred_element_type=jnp.float32
    )


def project_own_kernel(own, w_ref, unread, sum_ref, rest_ref):
    columns = own.shape[1]
    sum_ref[...] = weight_product(w_ref[:, part_columns(0, columns)], own)
    for k in range(1, NY):
        rest_ref[k - 1] = w_ref[:, part_columns(k, columns)]


def project_near_kernel(one, three, rest, sum_ref, out_ref):
    out_ref[...] = (
        sum_ref[...] + weight_product(rest[0], one) + weight_product(rest[2], three)
    )


def project_far_kernel(part, rest, sum_ref, *refs):
    out_ref = refs[-1]
    out_ref[...] = (sum_ref[...] + weight_product(rest[1], part)).T.astype(jnp.bfloat16)


def project_call(body, name, outs, flops, operands, unread=()):
    specs = [VMEM] * len(operands) + [pl.BlockSpec(memory_space=pl.ANY)] * len(unread)
    return pl.pallas_call(
        body,
        out_shape=tuple(jax.ShapeDtypeStruct(s, d) for s, d in outs),
        in_specs=specs,
        out_specs=tuple(VMEM for _ in outs),
        compiler_params=pltpu.CompilerParams(vmem_limit_bytes=24 * 1024 * 1024),
        cost_estimate=pl.CostEstimate(flops=flops, bytes_accessed=10**6, transcendentals=0),
        name=name,
    )(*operands, *unread)


SMEM = pl.BlockSpec(memory_space=pltpu.SMEM)
VMEM = pl.BlockSpec(memory_space=pltpu.VMEM)


def kernel_call(body, name, outs, scratch, flops, *operands):
    return pl.pallas_call(
        body,
        out_shape=tuple(jax.ShapeDtypeStruct(s, d) for s, d in outs),
        in_specs=[SMEM] + [VMEM] * (len(operands) - 1),
        out_specs=tuple(VMEM for _ in outs),
        scratch_shapes=[pltpu.VMEM(s, d) for s, d in scratch],
        compiler_params=pltpu.CompilerParams(vmem_limit_bytes=40 * 1024 * 1024),
        cost_estimate=pl.CostEstimate(flops=flops, bytes_accessed=10**6, transcendentals=0),
        name=name,
    )(*operands)


def spread_kernel(keys, values, copies):
    for k in range(NZ):
        copies[k, :, 0:HEAD] = keys[...]
        copies[k, :, HEAD:2 * HEAD] = values[...]


def after_kernel(*refs):
    pass


def after(value, *others):
    anywhere = pl.BlockSpec(memory_space=pl.ANY)
    return pl.pallas_call(
        after_kernel,
        out_shape=jax.ShapeDtypeStruct(value.shape, value.dtype),
        in_specs=[anywhere] * (1 + len(others)),
        out_specs=anywhere,
        input_output_aliases={0: 0},
        name="after",
    )(value, *others)


def shift(value, axis, distance):
    size = lax.axis_size(axis)
    return lax.ppermute(value, axis, [(i, (i + distance) % size) for i in range(size)])


def wide(value):
    return value.astype(jnp.float32)


def shards(queries, keys, values, out_grad, out_weight, pair_order):
    table = tables(pair_order)
    bf16, f32 = jnp.bfloat16, jnp.float32

    parts = {k: shift(out_grad, "y", k) for k in (1, 3, 2)}
    copies = pl.pallas_call(
        spread_kernel,
        out_shape=jax.ShapeDtypeStruct((NZ, 2 * SPAN, 2 * HEAD), bf16),
        in_specs=[VMEM, VMEM],
        out_specs=VMEM,
        cost_estimate=pl.CostEstimate(flops=SPREAD_FLOPS, bytes_accessed=10**6, transcendentals=0),
        name="spread",
    )(keys, values)
    rows, columns = out_grad.shape
    heads = out_weight.shape[0]
    summed, rest = project_call(
        project_own_kernel, "project_own", [((heads, rows), f32), ((NY - 1, heads, columns), bf16)],
        3 * 10**8, [out_grad, out_weight], [copies],
    )
    all_queries = [queries] + [shift(queries, "x", k) for k in (1, 2, 3)]
    (summed,) = project_call(
        project_near_kernel, "project_near", [((heads, rows), f32)], 6 * 10**8,
        [parts[1], parts[3], rest, summed],
    )
    (head_grads,) = project_call(
        project_far_kernel, "project_far", [((rows, heads), bf16)], 3 * 10**8,
        [parts[2], rest, summed], [table],
    )

    along_z = lax.all_to_all(copies, "z", 0, 0, tiled=True)
    along_z = after(along_z, head_grads, all_queries[1], all_queries[3])
    chunks = [along_z, shift(along_z, "c", 1)]

    kv, q_n, q_t, stats, o_t = kernel_call(
        forward_kernel, "forward",
        [((KEYS, 2 * HEAD), bf16), ((QSETS + 1, ROWS, HEAD), bf16), ((QSETS + 1, HEAD, ROWS), bf16),
         ((2, QSETS + 1, 8, ROWS), f32), ((QSETS + 1, HEAD, ROWS), f32)],
        [((QSETS + 1, 8, ROWS), f32)],
        4 * 10**9, table, *all_queries, *chunks,
    )
    all_grads = [head_grads] + [shift(head_grads, "x", k) for k in (1, 2, 3)]
    g_n, g_t, stats = kernel_call(
        weight_kernel, "weights",
        [((QSETS + 1, ROWS, HEAD), bf16), ((QSETS + 1, HEAD, ROWS), bf16), ((3, QSETS, ROWS), f32)],
        [], 10**7, table, *all_grads, stats, o_t,
    )
    all_stats = [stats] + [shift(stats, "x", k) for k in (1, 2, 3)]
    query_own, query_parts, terms = kernel_call(
        backward_kernel, "backward",
        [((2 * SPAN, HEADS * HEAD), f32), ((NX - 1, 2 * SPAN, HEADS * HEAD), bf16),
         ((KEY_DEVICES, 2 * SPAN, 2 * HEAD), bf16)],
        [((KEYS, 2 * HEAD), f32), ((QSETS + 1, HEAD, ROWS), f32), ((QSETS + 1, 8, ROWS), f32),
         ((QSETS + 1, 8, ROWS), f32)],
        8 * 10**9, table, *all_stats, kv, q_n, q_t, g_n, g_t,
    )
    query_gradient = query_own
    for k in (1, 2, 3):
        query_gradient = query_gradient + wide(shift(query_parts[k - 1], "x", k))

    terms = terms.reshape(NC, NZ, 2 * SPAN, 2 * HEAD)
    total = wide(terms[0]) + wide(shift(terms[1], "c", 1))
    total = lax.all_to_all(total.astype(bf16), "z", 0, 0, tiled=True)
    total = jnp.sum(wide(total), axis=0)
    return query_gradient, total[:, :HEAD], total[:, HEAD:]


def solution(mesh):
    split = Mesh(mesh.devices.reshape(NZ, NX, NC, NY), ("z", "x", "c", "y"))
    ctx = ("z", "x", "c")
    return jax.shard_map(
        shards,
        mesh=split,
        in_specs=(P(ctx, "y"), P(ctx, "y"), P(ctx, "y"), P(ctx, "y"), P("y", None), P()),
        out_specs=(P(ctx, "y"), P(ctx, "y"), P(ctx, "y")),
        check_vma=False,
    )
```

time: 667 us -> 111 us (0.17)
  waiting for transfers between devices: 464 us -> 23 us
  matrix products: 146 us -> 0 us
  starting transfers between devices: 0.19 us -> 41.4 us
  Pallas kernels: 0 us -> 32.7 us
  other arithmetic: 31.4 us -> 1.82 us
  between operations: 14.5 us -> 0.82 us
  local copies, waits for them, and re-layouts: 2.97 us -> 10.6 us
    reduce_scatter x2 -> x0, waiting for transfers between devices: 282 us -> none  [the longest x1 147 us: shards(): lax.psum_scatter(key_parts, 'ctx', scatter_dimension=0, tiled=True)]
    all_gather x3 -> x0, waiting for transfers between devices: 179 us -> none  [the longest x1 77.7 us: shards(): lax.all_gather(values, 'ctx', axis=0, tiled=True)]
    dot_general x113 -> x0, matrix products: 146 us -> none  [the longest x32 42.6 us: attention_scores(): jnp.einsum('qhd,kd->hqk', query_part, key_block, preferred_element_type=j...]
    pallas_call x0 -> x9, Pallas kernels: none -> 32.7 us  [the longest x3 25.6 us: kernel_call(): pl.pallas_call(body, out_shape=tuple((jax.ShapeDtypeStruct(s, d) for s, d...]
    ppermute x0 -> x17, starting transfers between devices: none -> 26.4 us  [shift(): lax.ppermute(value, axis, [(i, (i + distance) % size) for i in range(size)])]
    add x49 -> x1, other arithmetic: 21.1 us -> 0.83 us  [shards(): query_gradient = query_gradient + wide(shift(query_parts[k - 1], 'x', k))]
    ppermute x0 -> x17, waiting for transfers between devices: none -> 17.9 us  [shift(): lax.ppermute(value, axis, [(i, (i + distance) % size) for i in range(size)])]
    all_to_all x0 -> x2, starting transfers between devices: none -> 15 us  [the longest x1 9.01 us: shards(): along_z = lax.all_to_all(copies, 'z', 0, 0, tiled=True)]
  transfers between devices with their start and end apart: 5 -> 19, of which waited for: 5 -> 8; matrix products, arithmetic and copies ran while one was open for 2% -> 1% of each run, Pallas kernels for 0% -> 15%
where the time goes in v2:
time: 111 us; the launch traced here: 110 us
  starting transfers between devices  41.4 us (37%)
  Pallas kernels  32.7 us (29%)
  waiting for transfers between devices  23 us (21%)
  local copies, waits for them, and re-layouts  10.6 us (10%)
  other arithmetic  1.82 us (2%)
    ppermute x17, starting transfers between devices, shift(): lax.ppermute(value, axis, [(i, (i + distance) % size) for i in range(size)])  26.4 us
    pallas_call x3, Pallas kernels, kernel_call(): pl.pallas_call(body, out_shape=tuple((jax.ShapeDtypeStruct(s, d) for s, d...  25.6 us
    ppermute x17, waiting for transfers between devices, shift(): lax.ppermute(value, axis, [(i, (i + distance) % size) for i in range(size)])  17.9 us
    unnamed x26, local copies, waits for them, and re-layouts  9.83 us
    all_to_all x1, starting transfers between devices, shards(): along_z = lax.all_to_all(copies, 'z', 0, 0, tiled=True)  9.01 us
    all_to_all x1, starting transfers between devices, shards(): total = lax.all_to_all(total.astype(bf16), 'z', 0, 0, tiled=True)  6.01 us
    all_to_all x1, waiting for transfers between devices, shards(): total = lax.all_to_all(total.astype(bf16), 'z', 0, 0, tiled=True)  5.07 us
    pallas_call x3, Pallas kernels, project_call(): pl.pallas_call(body, out_shape=tuple((jax.ShapeDtypeStruct(s, d) for s, d...  3.42 us
  transfers between devices with their start and end apart: 19, of which 8 were waited for; matrix products, arithmetic and copies ran while one was open for 1% of the time, Pallas kernels for 15%

profile of v2, /device:TPU:1, one launch (start us, length us, event | category | flops | bytes accessed | tf_op | source)
XLA Modules:
  0.0 110.3 jit_solution(10219591221139348204)
XLA Ops:
  0.6 0.0 copy-start.6
  0.6 0.0 copy-start.12
  0.7 1.7 %spread.1.unread = bf16[8,128,256]{2,1,0:T(8,128)(2,1)} custom-call(bf16[128,128]{1,0:T(8,128)(2,1)} %keys.1, bf16[128,128]{1,0:T(8,128)(2,1)} %values.1), custom_call_target="tpu_custom_call" | custom-call | flops 20000000000 | bytes 1000000 | tf_op jit(solution)/shard_map/spread/pallas_call | solution.py:338
  2.3 9.0 %all-to-all-start = ((bf16[8,128,256]{2,1,0:T(8,128)(2,1)}), bf16[8,128,256]{2,1,0:T(8,128)(2,1)S(1)}, u32[]{:S(2)}, u32[]{:S(2)}) async-start(bf16[8,128,256]{2,1,0:T(8,128)(2,1)} %spread.1.unread), calls=%async_computation | async-start | bytes 1048576 | tf_op jit(solution)/shard_map/all_to_all | solution.py:362
  11.4 0.0 copy-done.6
  11.4 1.4 %collective-permute-start.1 = (bf16[128,1536]{1,0:T(8,128)(2,1)S(1)}, bf16[128,1536]{1,0:T(8,128)(2,1)S(1)}, u32[]{:S(2)}, u32[]{:S(2)}) collective-permute-start(bf16[128,1536]{1,0:T(8,128)(2,1)S(1)} %copy-done.6), channel_id=1, source_target_pairs={{0,1},{1,2},{2,3},{3,0},{4,5},{5,6},{6,7},{7,4},{8,9},{9,10},{10,1... | collective-permute-start | bytes 1179656 | tf_op jit(solution)/shard_map/ppermute | solution.py:326
  12.7 1.5 %collective-permute-start.2 = (bf16[128,1536]{1,0:T(8,128)(2,1)S(1)}, bf16[128,1536]{1,0:T(8,128)(2,1)S(1)}, u32[]{:S(2)}, u32[]{:S(2)}) collective-permute-start(bf16[128,1536]{1,0:T(8,128)(2,1)S(1)} %copy-done.6), channel_id=1, source_target_pairs={{0,3},{1,0},{2,1},{3,2},{4,7},{5,4},{6,5},{7,6},{8,11},{9,8},{10,9... | collective-permute-start | bytes 1179656 | tf_op jit(solution)/shard_map/ppermute | solution.py:326
  14.3 1.6 %collective-permute-start = (bf16[128,1536]{1,0:T(8,128)(2,1)S(1)}, bf16[128,1536]{1,0:T(8,128)(2,1)S(1)}, u32[]{:S(2)}, u32[]{:S(2)}) collective-permute-start(bf16[128,1536]{1,0:T(8,128)(2,1)S(1)} %copy-done.6), channel_id=1, source_target_pairs={{0,2},{1,3},{2,0},{3,1},{4,6},{5,7},{6,4},{7,5},{8,10},{9,11},{10,... | collective-permute-start | bytes 1179656 | tf_op jit(solution)/shard_map/ppermute | solution.py:326
  15.8 1.2 %collective-permute-start.6 = (bf16[128,768]{1,0:T(8,128)(2,1)S(1)}, bf16[128,768]{1,0:T(8,128)(2,1)S(1)}, u32[]{:S(2)}, u32[]{:S(2)}) collective-permute-start(bf16[128,768]{1,0:T(8,128)(2,1)S(1)} %copy-done.12), channel_id=1, source_target_pairs={{0,8},{8,16},{16,24},{24,0},{1,9},{9,17},{17,25},{25,1},{2,10},{10... | collective-permute-start | bytes 589832 | tf_op jit(solution)/shard_map/ppermute | solution.py:326
  17.0 1.5 %collective-permute-start.8 = (bf16[128,768]{1,0:T(8,128)(2,1)S(1)}, bf16[128,768]{1,0:T(8,128)(2,1)S(1)}, u32[]{:S(2)}, u32[]{:S(2)}) collective-permute-start(bf16[128,768]{1,0:T(8,128)(2,1)S(1)} %copy-done.12), channel_id=1, source_target_pairs={{0,24},{8,0},{16,8},{24,16},{1,25},{9,1},{17,9},{25,17},{2,26},{10... | collective-permute-start | bytes 589832 | tf_op jit(solution)/shard_map/ppermute | solution.py:326
  18.5 2.1 %tables.1.refs_0_.table = s32[192]{0:T(256)} custom-call(s32[64]{0:T(128)} %pair.1), custom_call_target="tpu_custom_call" | custom-call | flops 1000000 | bytes 1000 | tf_op jit(solution)/shard_map/tables/pallas_call | solution.py:77
  20.6 0.0 copy-start
  20.6 3.7 %copy-done = bf16[768,6144]{1,0:T(8,128)(2,1)S(1)} copy-done((bf16[768,6144]{1,0:T(8,128)(2,1)S(1)}, bf16[768,6144]{1,0:T(8,128)(2,1)}, u32[]{:S(2)}) %copy-start) | copy-done | bytes 9437208
  24.3 1.0 copy-done.3
  25.3 1.2 %project_own.1 = (f32[768,128]{1,0:T(8,128)S(1)}, bf16[3,768,1536]{2,1,0:T(8,128)(2,1)S(1)}) custom-call(bf16[128,1536]{1,0:T(8,128)(2,1)S(1)} %copy-done.6, bf16[768,6144]{1,0:T(8,128)(2,1)S(1)} %copy-done, bf16[8,128,256]{2,1,0:T(8,128)(2,1)S(1)} %copy-done.3), custom_call_target="tpu_custom_call" | custom-call | flops 300000000 | bytes 1000000 | tf_op jit(solution)/shard_map/project_own/pallas_call | solution.py:274
  26.5 0.0 collective-permute-done.1.one
  26.5 0.0 collective-permute-done.2.three
  26.5 1.4 %project_near.1.sum_ref = f32[768,128]{1,0:T(8,128)S(1)} custom-call(bf16[128,1536]{1,0:T(8,128)(2,1)S(1)} %collective-permute-done.1.one, bf16[128,1536]{1,0:T(8,128)(2,1)S(1)} %collective-permute-done.2.three, bf16[3,768,1536]{2,1,0:T(8,128)(2,1)S(1)} %get-tuple-element.16.rest, f32[768,128]{1,0:T(8,128)S(1)} %get-tuple-element.17.sum_ref), custom_call_target="tpu_custom_call" | custom-call | flops 600000000 | bytes 1000000 | tf_op jit(solution)/shard_map/project_near/pallas_call | solution.py:274
  27.9 4.1 %collective-permute-done.part = bf16[128,1536]{1,0:T(8,128)(2,1)S(1)} collective-permute-done((bf16[128,1536]{1,0:T(8,128)(2,1)S(1)}, bf16[128,1536]{1,0:T(8,128)(2,1)S(1)}, u32[]{:S(2)}, u32[]{:S(2)}) %collective-permute-start) | collective-permute-done | bytes 393248 | tf_op jit(solution)/shard_map/ppermute | solution.py:326
  32.0 0.8 project_far.1.refs_1_.refs_0_
  32.8 0.0 copy-start.4
  32.9 0.7 copy-done.4
  33.5 0.0 collective-permute-done.6.refs_2_.refs_1_
  33.5 0.0 collective-permute-done.8.refs_3_
  33.5 0.0 all-to-all-done.refs_0_
  33.6 0.7 copy-done.7
  34.2 0.1 copy-done.9
  34.3 0.8 copy-done.1
  35.1 1.9 %collective-permute-start.9 = (bf16[8,128,256]{2,1,0:T(8,128)(2,1)}, bf16[8,128,256]{2,1,0:T(8,128)(2,1)S(1)}, u32[]{:S(2)}, u32[]{:S(2)}) collective-permute-start(bf16[8,128,256]{2,1,0:T(8,128)(2,1)} %after.1.refs_4_), channel_id=1, source_target_pairs={{0,4},{4,0},{1,5},{5,1},{2,6},{6,2},{3,7},{7,3},{8,12},{12,8},{9,1... | collective-permute-start | bytes 1572872 | tf_op jit(solution)/shard_map/ppermute | solution.py:326
  36.9 2.8 %collective-permute-start.7 = (bf16[128,768]{1,0:T(8,128)(2,1)S(1)}, bf16[128,768]{1,0:T(8,128)(2,1)S(1)}, u32[]{:S(2)}, u32[]{:S(2)}) collective-permute-start(bf16[128,768]{1,0:T(8,128)(2,1)S(1)} %copy-done.12), channel_id=1, source_target_pairs={{0,16},{8,24},{16,0},{24,8},{1,17},{9,25},{17,1},{25,9},{2,18},{10... | collective-permute-start | bytes 589832 | tf_op jit(solution)/shard_map/ppermute | solution.py:326
  39.7 0.3 collective-permute-start.3
  40.0 1.7 %collective-permute-start.4 = (bf16[128,768]{1,0:T(8,128)(2,1)}, bf16[128,768]{1,0:T(8,128)(2,1)S(1)}, u32[]{:S(2)}, u32[]{:S(2)}) collective-permute-start(bf16[128,768]{1,0:T(8,128)(2,1)} %copy-done.4), channel_id=1, source_target_pairs={{0,16},{8,24},{16,0},{24,8},{1,17},{9,25},{17,1},{25,9},{2,18},{10... | collective-permute-start | bytes 589832 | tf_op jit(solution)/shard_map/ppermute | solution.py:326
  41.7 0.7 collective-permute-start.5
  42.4 2.6 %collective-permute-done.7.refs_2_ = bf16[128,768]{1,0:T(8,128)(2,1)S(1)} collective-permute-done((bf16[128,768]{1,0:T(8,128)(2,1)S(1)}, bf16[128,768]{1,0:T(8,128)(2,1)S(1)}, u32[]{:S(2)}, u32[]{:S(2)}) %collective-permute-start.7) | collective-permute-done | bytes 196640 | tf_op jit(solution)/shard_map/ppermute | solution.py:326
  45.0 0.0 collective-permute-done.9.refs_5_
  45.0 1.0 copy-done.2
  46.0 0.9 copy-done.8
  47.0 0.9 copy-done.10
  47.9 11.1 %forward.1 = (bf16[2048,256]{1,0:T(8,128)(2,1)S(1)}, bf16[9,384,128]{2,1,0:T(8,128)(2,1)S(1)}, bf16[9,128,384]{2,1,0:T(8,128)(2,1)S(1)}, f32[2,9,8,384]{3,2,1,0:T(8,128)S(1)}, f32[9,128,384]{2,1,0:T(8,128)S(1)}) custom-call(s32[192]{0:T(256)S(1)} %copy-done.11, bf16[128,768]{1,0:T(8,128)(2,1)S(1)} %copy-done.12, bf16[128,768]{1,0:T(8,128)(2,1)S(1)} %copy-done.8, ...), custom_call_target="tpu_custom_call" | custom-call | flops 4000000000 | bytes 1000000 | tf_op jit(solution)/shard_map/forward/pallas_call | solution.py:290
  59.0 0.0 collective-permute-done.3.refs_1_
  59.0 0.0 collective-permute-done.4.refs_2_
  59.0 0.0 collective-permute-done.5.refs_3_
  59.0 0.9 weights.1
  59.9 1.3 %collective-permute-start.10 = (f32[3,8,384]{2,1,0:T(8,128)S(1)}, f32[3,8,384]{2,1,0:T(8,128)S(1)}, u32[]{:S(2)}, u32[]{:S(2)}) collective-permute-start(f32[3,8,384]{2,1,0:T(8,128)S(1)} %get-tuple-element.20.refs_0_), channel_id=1, source_target_pairs={{0,8},{8,16},{16,24},{24,0},{1,9},{9,17},{17,25},{25,1},{2,10},{10... | collective-permute-start | bytes 110600 | tf_op jit(solution)/shard_map/ppermute | solution.py:326
  61.2 1.9 %collective-permute-start.11 = (f32[3,8,384]{2,1,0:T(8,128)S(1)}, f32[3,8,384]{2,1,0:T(8,128)S(1)}, u32[]{:S(2)}, u32[]{:S(2)}) collective-permute-start(f32[3,8,384]{2,1,0:T(8,128)S(1)} %get-tuple-element.20.refs_0_), channel_id=1, source_target_pairs={{0,16},{8,24},{16,0},{24,8},{1,17},{9,25},{17,1},{25,9},{2,18},{10... | collective-permute-start | bytes 110600 | tf_op jit(solution)/shard_map/ppermute | solution.py:326
  63.1 1.8 %collective-permute-start.12 = (f32[3,8,384]{2,1,0:T(8,128)S(1)}, f32[3,8,384]{2,1,0:T(8,128)S(1)}, u32[]{:S(2)}, u32[]{:S(2)}) collective-permute-start(f32[3,8,384]{2,1,0:T(8,128)S(1)} %get-tuple-element.20.refs_0_), channel_id=1, source_target_pairs={{0,24},{8,0},{16,8},{24,16},{1,25},{9,1},{17,9},{25,17},{2,26},{10... | collective-permute-start | bytes 110600 | tf_op jit(solution)/shard_map/ppermute | solution.py:326
  64.9 0.0 collective-permute-done.10.refs_1_
  64.9 0.7 collective-permute-done.11.refs_2_
  65.6 0.6 collective-permute-done.12.refs_3_
  66.2 13.6 %backward.1 = (f32[128,768]{1,0:T(8,128)S(1)}, bf16[3,128,768]{2,1,0:T(8,128)(2,1)S(1)}, bf16[16,128,256]{2,1,0:T(8,128)(2,1)S(1)}) custom-call(s32[192]{0:T(256)S(1)} %copy-done.11, f32[3,8,384]{2,1,0:T(8,128)S(1)} %get-tuple-element.20.refs_0_, f32[3,8,384]{2,1,0:T(8,128)S(1)} %collective-permute-done.10.refs_1_, ...), custom_call_target="tpu_custom_call" | custom-call | flops 8000000000 | bytes 1000000 | tf_op jit(solution)/shard_map/backward/pallas_call | solution.py:290
  79.8 3.3 %collective-permute-start.16 = (bf16[8,128,256]{2,1,0:T(8,128)(2,1)S(1)}, bf16[8,128,256]{2,1,0:T(8,128)(2,1)S(1)}, u32[]{:S(2)}, u32[]{:S(2)}) collective-permute-start(bf16[8,128,256]{2,1,0:T(8,128)(2,1)S(1)} %slice.27), channel_id=1, source_target_pairs={{0,4},{4,0},{1,5},{5,1},{2,6},{6,2},{3,7},{7,3},{8,12},{12,8},{9,1... | collective-permute-start | bytes 1572872 | tf_op jit(solution)/shard_map/ppermute | solution.py:326
  83.2 1.5 %collective-permute-done.16 = bf16[8,128,256]{2,1,0:T(8,128)(2,1)S(1)} collective-permute-done((bf16[8,128,256]{2,1,0:T(8,128)(2,1)S(1)}, bf16[8,128,256]{2,1,0:T(8,128)(2,1)S(1)}, u32[]{:S(2)}, u32[]{:S(2)}) %collective-permute-start.16) | collective-permute-done | bytes 524320 | tf_op jit(solution)/shard_map/ppermute | solution.py:326
  84.7 0.9 add_convert_fusion
  85.6 6.0 %all-to-all-start.1 = ((bf16[8,128,256]{2,1,0:T(8,128)(2,1)}), bf16[8,128,256]{2,1,0:T(8,128)(2,1)S(1)}, u32[]{:S(2)}, u32[]{:S(2)}) async-start(bf16[8,128,256]{2,1,0:T(8,128)(2,1)} %add_convert_fusion), calls=%async_computation.1 | async-start | bytes 1048576 | tf_op jit(solution)/shard_map/all_to_all | solution.py:394
  91.7 0.6 collective-permute-start.13
  92.2 2.9 %collective-permute-start.14 = (bf16[128,768]{1,0:T(8,128)(2,1)S(1)}, bf16[128,768]{1,0:T(8,128)(2,1)S(1)}, u32[]{:S(2)}, u32[]{:S(2)}) collective-permute-start(bf16[128,768]{1,0:T(8,128)(2,1)S(1)} %get-tuple-element.31), channel_id=1, source_target_pairs={{0,16},{8,24},{16,0},{24,8},{1,17},{9,25},{17,1},{25,9},{2,18},{10... | collective-permute-start | bytes 589832 | tf_op jit(solution)/shard_map/ppermute | solution.py:326
  95.1 0.2 collective-permute-start.15
  95.3 3.4 %collective-permute-done.13 = bf16[128,768]{1,0:T(8,128)(2,1)S(1)} collective-permute-done((bf16[128,768]{1,0:T(8,128)(2,1)S(1)}, bf16[128,768]{1,0:T(8,128)(2,1)S(1)}, u32[]{:S(2)}, u32[]{:S(2)}) %collective-permute-start.13) | collective-permute-done | bytes 196640 | tf_op jit(solution)/shard_map/ppermute | solution.py:326
  98.7 4.9 %collective-permute-done.14 = bf16[128,768]{1,0:T(8,128)(2,1)S(1)} collective-permute-done((bf16[128,768]{1,0:T(8,128)(2,1)S(1)}, bf16[128,768]{1,0:T(8,128)(2,1)S(1)}, u32[]{:S(2)}, u32[]{:S(2)}) %collective-permute-start.14) | collective-permute-done | bytes 196640 | tf_op jit(solution)/shard_map/ppermute | solution.py:326
  103.7 0.0 collective-permute-done.15
  103.7 0.8 convert_add_fusion
  104.5 5.1 %all-to-all-done.1 = bf16[8,128,256]{2,1,0:T(8,128)(2,1)S(1)} async-done(((bf16[8,128,256]{2,1,0:T(8,128)(2,1)}), bf16[8,128,256]{2,1,0:T(8,128)(2,1)S(1)}, u32[]{:S(2)}, u32[]{:S(2)}) %all-to-all-start.1) | async-done | bytes 524320 | tf_op jit(solution)/shard_map/all_to_all | solution.py:394
  109.6 0.1 convert_reduce_fusion
  109.7 0.7 fusion
  (15 shorter events, 0.1 us)
Async XLA Ops:
  0.6 10.7 %copy-start.6 = (bf16[128,1536]{1,0:T(8,128)(2,1)S(1)}, bf16[128,1536]{1,0:T(8,128)(2,1)}, u32[]{:S(2)}) copy-start(bf16[128,1536]{1,0:T(8,128)(2,1)} %own.1) | copy-start | bytes 1179652
  0.6 15.2 %copy-start.12 = (bf16[128,768]{1,0:T(8,128)(2,1)S(1)}, bf16[128,768]{1,0:T(8,128)(2,1)}, u32[]{:S(2)}) copy-start(bf16[128,768]{1,0:T(8,128)(2,1)} %refs_0_.1) | copy-start | bytes 589828
  2.3 31.2 %all-to-all-start = ((bf16[8,128,256]{2,1,0:T(8,128)(2,1)}), bf16[8,128,256]{2,1,0:T(8,128)(2,1)S(1)}, u32[]{:S(2)}, u32[]{:S(2)}) async-start(bf16[8,128,256]{2,1,0:T(8,128)(2,1)} %spread.1.unread), calls=%async_computation | async-start | bytes 1048576 | tf_op jit(solution)/shard_map/all_to_all | solution.py:362
  11.4 15.1 %collective-permute-start.1 = (bf16[128,1536]{1,0:T(8,128)(2,1)S(1)}, bf16[128,1536]{1,0:T(8,128)(2,1)S(1)}, u32[]{:S(2)}, u32[]{:S(2)}) collective-permute-start(bf16[128,1536]{1,0:T(8,128)(2,1)S(1)} %copy-done.6), channel_id=1, source_target_pairs={{0,1},{1,2},{2,3},{3,0},{4,5},{5,6},{6,7},{7,4},{8,9},{9,10},{10,1... | collective-permute-start | bytes 1179656 | tf_op jit(solution)/shard_map/ppermute | solution.py:326
  12.7 13.8 %collective-permute-start.2 = (bf16[128,1536]{1,0:T(8,128)(2,1)S(1)}, bf16[128,1536]{1,0:T(8,128)(2,1)S(1)}, u32[]{:S(2)}, u32[]{:S(2)}) collective-permute-start(bf16[128,1536]{1,0:T(8,128)(2,1)S(1)} %copy-done.6), channel_id=1, source_target_pairs={{0,3},{1,0},{2,1},{3,2},{4,7},{5,4},{6,5},{7,6},{8,11},{9,8},{10,9... | collective-permute-start | bytes 1179656 | tf_op jit(solution)/shard_map/ppermute | solution.py:326
  14.3 17.7 %collective-permute-start = (bf16[128,1536]{1,0:T(8,128)(2,1)S(1)}, bf16[128,1536]{1,0:T(8,128)(2,1)S(1)}, u32[]{:S(2)}, u32[]{:S(2)}) collective-permute-start(bf16[128,1536]{1,0:T(8,128)(2,1)S(1)} %copy-done.6), channel_id=1, source_target_pairs={{0,2},{1,3},{2,0},{3,1},{4,6},{5,7},{6,4},{7,5},{8,10},{9,11},{10,... | collective-permute-start | bytes 1179656 | tf_op jit(solution)/shard_map/ppermute | solution.py:326
  15.8 17.7 %collective-permute-start.6 = (bf16[128,768]{1,0:T(8,128)(2,1)S(1)}, bf16[128,768]{1,0:T(8,128)(2,1)S(1)}, u32[]{:S(2)}, u32[]{:S(2)}) collective-permute-start(bf16[128,768]{1,0:T(8,128)(2,1)S(1)} %copy-done.12), channel_id=1, source_target_pairs={{0,8},{8,16},{16,24},{24,0},{1,9},{9,17},{17,25},{25,1},{2,10},{10... | collective-permute-start | bytes 589832 | tf_op jit(solution)/shard_map/ppermute | solution.py:326
  17.0 16.5 %collective-permute-start.8 = (bf16[128,768]{1,0:T(8,128)(2,1)S(1)}, bf16[128,768]{1,0:T(8,128)(2,1)S(1)}, u32[]{:S(2)}, u32[]{:S(2)}) collective-permute-start(bf16[128,768]{1,0:T(8,128)(2,1)S(1)} %copy-done.12), channel_id=1, source_target_pairs={{0,24},{8,0},{16,8},{24,16},{1,25},{9,1},{17,9},{25,17},{2,26},{10... | collective-permute-start | bytes 589832 | tf_op jit(solution)/shard_map/ppermute | solution.py:326
  20.6 3.7 %copy-start = (bf16[768,6144]{1,0:T(8,128)(2,1)S(1)}, bf16[768,6144]{1,0:T(8,128)(2,1)}, u32[]{:S(2)}) copy-start(bf16[768,6144]{1,0:T(8,128)(2,1)} %w_ref.1) | copy-start | bytes 28311556
  24.3 1.0 copy-start.3
  25.3 6.7 %copy-start.11 = (s32[192]{0:T(256)S(1)}, s32[192]{0:T(256)}, u32[]{:S(2)}) copy-start(s32[192]{0:T(256)} %tables.1.refs_0_.table) | copy-start | bytes 2308
  32.8 0.7 copy-start.4
  33.5 0.7 copy-start.7
  33.5 0.8 copy-start.9
  34.3 0.8 copy-start.1
  35.1 23.9 %copy-start.5 = (bf16[128,768]{1,0:T(8,128)(2,1)S(1)}, bf16[128,768]{1,0:T(8,128)(2,1)}, u32[]{:S(2)}) copy-start(bf16[128,768]{1,0:T(8,128)(2,1)} %copy-done.4) | copy-start | bytes 589828
  35.1 9.9 %collective-permute-start.9 = (bf16[8,128,256]{2,1,0:T(8,128)(2,1)}, bf16[8,128,256]{2,1,0:T(8,128)(2,1)S(1)}, u32[]{:S(2)}, u32[]{:S(2)}) collective-permute-start(bf16[8,128,256]{2,1,0:T(8,128)(2,1)} %after.1.refs_4_), channel_id=1, source_target_pairs={{0,4},{4,0},{1,5},{5,1},{2,6},{6,2},{3,7},{7,3},{8,12},{12,8},{9,1... | collective-permute-start | bytes 1572872 | tf_op jit(solution)/shard_map/ppermute | solution.py:326
  36.9 8.0 %collective-permute-start.7 = (bf16[128,768]{1,0:T(8,128)(2,1)S(1)}, bf16[128,768]{1,0:T(8,128)(2,1)S(1)}, u32[]{:S(2)}, u32[]{:S(2)}) collective-permute-start(bf16[128,768]{1,0:T(8,128)(2,1)S(1)} %copy-done.12), channel_id=1, source_target_pairs={{0,16},{8,24},{16,0},{24,8},{1,17},{9,25},{17,1},{25,9},{2,18},{10... | collective-permute-start | bytes 589832 | tf_op jit(solution)/shard_map/ppermute | solution.py:326
  39.7 19.3 %collective-permute-start.3 = (bf16[128,768]{1,0:T(8,128)(2,1)}, bf16[128,768]{1,0:T(8,128)(2,1)S(1)}, u32[]{:S(2)}, u32[]{:S(2)}) collective-permute-start(bf16[128,768]{1,0:T(8,128)(2,1)} %copy-done.4), channel_id=1, source_target_pairs={{0,8},{8,16},{16,24},{24,0},{1,9},{9,17},{17,25},{25,1},{2,10},{10... | collective-permute-start | bytes 589832 | tf_op jit(solution)/shard_map/ppermute | solution.py:326
  40.0 19.0 %collective-permute-start.4 = (bf16[128,768]{1,0:T(8,128)(2,1)}, bf16[128,768]{1,0:T(8,128)(2,1)S(1)}, u32[]{:S(2)}, u32[]{:S(2)}) collective-permute-start(bf16[128,768]{1,0:T(8,128)(2,1)} %copy-done.4), channel_id=1, source_target_pairs={{0,16},{8,24},{16,0},{24,8},{1,17},{9,25},{17,1},{25,9},{2,18},{10... | collective-permute-start | bytes 589832 | tf_op jit(solution)/shard_map/ppermute | solution.py:326
  41.7 17.2 %collective-permute-start.5 = (bf16[128,768]{1,0:T(8,128)(2,1)}, bf16[128,768]{1,0:T(8,128)(2,1)S(1)}, u32[]{:S(2)}, u32[]{:S(2)}) collective-permute-start(bf16[128,768]{1,0:T(8,128)(2,1)} %copy-done.4), channel_id=1, source_target_pairs={{0,24},{8,0},{16,8},{24,16},{1,25},{9,1},{17,9},{25,17},{2,26},{10... | collective-permute-start | bytes 589832 | tf_op jit(solution)/shard_map/ppermute | solution.py:326
  45.0 1.0 copy-start.2
  46.0 0.9 copy-start.8
  47.0 0.9 copy-start.10
  59.9 5.0 %collective-permute-start.10 = (f32[3,8,384]{2,1,0:T(8,128)S(1)}, f32[3,8,384]{2,1,0:T(8,128)S(1)}, u32[]{:S(2)}, u32[]{:S(2)}) collective-permute-start(f32[3,8,384]{2,1,0:T(8,128)S(1)} %get-tuple-element.20.refs_0_), channel_id=1, source_target_pairs={{0,8},{8,16},{16,24},{24,0},{1,9},{9,17},{17,25},{25,1},{2,10},{10... | collective-permute-start | bytes 110600 | tf_op jit(solution)/shard_map/ppermute | solution.py:326
  61.2 4.3 %collective-permute-start.11 = (f32[3,8,384]{2,1,0:T(8,128)S(1)}, f32[3,8,384]{2,1,0:T(8,128)S(1)}, u32[]{:S(2)}, u32[]{:S(2)}) collective-permute-start(f32[3,8,384]{2,1,0:T(8,128)S(1)} %get-tuple-element.20.refs_0_), channel_id=1, source_target_pairs={{0,16},{8,24},{16,0},{24,8},{1,17},{9,25},{17,1},{25,9},{2,18},{10... | collective-permute-start | bytes 110600 | tf_op jit(solution)/shard_map/ppermute | solution.py:326
  63.1 3.1 %collective-permute-start.12 = (f32[3,8,384]{2,1,0:T(8,128)S(1)}, f32[3,8,384]{2,1,0:T(8,128)S(1)}, u32[]{:S(2)}, u32[]{:S(2)}) collective-permute-start(f32[3,8,384]{2,1,0:T(8,128)S(1)} %get-tuple-element.20.refs_0_), channel_id=1, source_target_pairs={{0,24},{8,0},{16,8},{24,16},{1,25},{9,1},{17,9},{25,17},{2,26},{10... | collective-permute-start | bytes 110600 | tf_op jit(solution)/shard_map/ppermute | solution.py:326
  79.8 4.9 %collective-permute-start.16 = (bf16[8,128,256]{2,1,0:T(8,128)(2,1)S(1)}, bf16[8,128,256]{2,1,0:T(8,128)(2,1)S(1)}, u32[]{:S(2)}, u32[]{:S(2)}) collective-permute-start(bf16[8,128,256]{2,1,0:T(8,128)(2,1)S(1)} %slice.27), channel_id=1, source_target_pairs={{0,4},{4,0},{1,5},{5,1},{2,6},{6,2},{3,7},{7,3},{8,12},{12,8},{9,1... | collective-permute-start | bytes 1572872 | tf_op jit(solution)/shard_map/ppermute | solution.py:326
  85.6 24.0 %all-to-all-start.1 = ((bf16[8,128,256]{2,1,0:T(8,128)(2,1)}), bf16[8,128,256]{2,1,0:T(8,128)(2,1)S(1)}, u32[]{:S(2)}, u32[]{:S(2)}) async-start(bf16[8,128,256]{2,1,0:T(8,128)(2,1)} %add_convert_fusion), calls=%async_computation.1 | async-start | bytes 1048576 | tf_op jit(solution)/shard_map/all_to_all | solution.py:394
  91.7 7.1 %collective-permute-start.13 = (bf16[128,768]{1,0:T(8,128)(2,1)S(1)}, bf16[128,768]{1,0:T(8,128)(2,1)S(1)}, u32[]{:S(2)}, u32[]{:S(2)}) collective-permute-start(bf16[128,768]{1,0:T(8,128)(2,1)S(1)} %get-tuple-element.29), channel_id=1, source_target_pairs={{0,8},{8,16},{16,24},{24,0},{1,9},{9,17},{17,25},{25,1},{2,10},{10... | collective-permute-start | bytes 589832 | tf_op jit(solution)/shard_map/ppermute | solution.py:326
  92.2 11.4 %collective-permute-start.14 = (bf16[128,768]{1,0:T(8,128)(2,1)S(1)}, bf16[128,768]{1,0:T(8,128)(2,1)S(1)}, u32[]{:S(2)}, u32[]{:S(2)}) collective-permute-start(bf16[128,768]{1,0:T(8,128)(2,1)S(1)} %get-tuple-element.31), channel_id=1, source_target_pairs={{0,16},{8,24},{16,0},{24,8},{1,17},{9,25},{17,1},{25,9},{2,18},{10... | collective-permute-start | bytes 589832 | tf_op jit(solution)/shard_map/ppermute | solution.py:326
  95.1 8.5 %collective-permute-start.15 = (bf16[128,768]{1,0:T(8,128)(2,1)S(1)}, bf16[128,768]{1,0:T(8,128)(2,1)S(1)}, u32[]{:S(2)}, u32[]{:S(2)}) collective-permute-start(bf16[128,768]{1,0:T(8,128)(2,1)S(1)} %get-tuple-element.30), channel_id=1, source_target_pairs={{0,24},{8,0},{16,8},{24,16},{1,25},{9,1},{17,9},{25,17},{2,26},{10... | collective-permute-start | bytes 589832 | tf_op jit(solution)/shard_map/ppermute | solution.py:326

commit v3 on v2

--- a/solution.py
+++ b/solution.py
@@ -20,13 +20,13 @@
 KEY_SPANS = 2 * KEY_DEVICES
 KEYS = KEY_SPANS * SPAN
 MAX_STEPS = 48
-T_RANK, T_SPAN, T_QSPAN, T_QSET, T_BLOCK, T_COUNT, T_X, T_C = (
-    0, 16, 48, 64, 112, 160, 161, 162
+T_RANK, T_SPAN, T_QSPAN, T_QSET, T_BLOCK, T_COUNT, T_X, T_C, T_FULL = (
+    0, 16, 48, 64, 112, 160, 161, 162, 163
 )
 TABLE = 192
 SPREAD_FLOPS = 2 * 10**10
 LOW = -1e30
-PAIR_STEPS = 2
+PAIR_STEPS = 4
 
 
 def table_kernel(pair, table):
@@ -45,6 +45,7 @@
     table[T_X] = x
     table[T_C] = c
     end = jnp.int32(0)
+    lasts = []
     for u in range(QSETS):
         low = pair[(z * NX + u // 2) * NC + c]
         below = jnp.int32(0)
@@ -58,19 +59,26 @@
         else:
             table[T_QSPAN + u] = SPANS - 1 - low
             seen = KEY_SPANS - below
-        count = (seen + PER_BLOCK - 1) // PER_BLOCK
+        last = (seen + PER_BLOCK - 1) // PER_BLOCK - 1
+        lasts.append(last)
 
         def fill(j, carry, u=u, end=end):
             table[T_QSET + end + j] = u
             table[T_BLOCK + end + j] = j
             return carry
 
-        lax.fori_loop(0, count, fill, 0)
-        end = end + count
-    table[T_COUNT] = end
+        lax.fori_loop(0, last, fill, 0)
+        end = end + jnp.maximum(last, 0)
+    table[T_FULL] = end // PAIR_STEPS * PAIR_STEPS
+    for u in range(QSETS):
+        none = lasts[u] < 0
+        table[T_QSET + end + u] = jnp.where(none, QSETS, u)
+        table[T_BLOCK + end + u] = jnp.maximum(lasts[u], 0)
+    table[T_COUNT] = end + QSETS
     table[T_QSPAN + QSETS] = -SPANS
-    table[T_QSET + end] = QSETS
-    table[T_BLOCK + end] = 0
+    for k in range(PAIR_STEPS - 1):
+        table[T_QSET + end + QSETS + k] = QSETS
+        table[T_BLOCK + end + QSETS + k] = 0
 
 
 def tables(pair_order):
@@ -84,8 +92,10 @@
     )(pair_order)
 
 
-def masked_scores(table, keys, q_t, u, j):
+def masked_scores(table, keys, q_t, u, j, masked):
     sc = jnp.dot(keys, q_t[u], preferred_element_type=jnp.float32)
+    if not masked:
+        return sc
     row = lax.broadcasted_iota(jnp.int32, (SPAN, ROWS), 0)
     col = lax.broadcasted_iota(jnp.int32, (SPAN, ROWS), 1) % SPAN
     ahead = row - col
@@ -95,6 +105,13 @@
         room = (q_span - table[T_SPAN + j * PER_BLOCK + i]) * SPAN
         pieces.append(jnp.where(ahead <= room, sc[i * SPAN:(i + 1) * SPAN, :], -jnp.inf))
     return jnp.concatenate(pieces, axis=0)
+
+
+def step_loops(table, body):
+    full = table[T_FULL] // PAIR_STEPS
+    end = (table[T_COUNT] + PAIR_STEPS - 1) // PAIR_STEPS
+    lax.fori_loop(0, full, lambda i, carry: body(i, carry, False), 0)
+    lax.fori_loop(full, end, lambda i, carry: body(i, carry, True), 0)
 
 
 def block_rows(j):
@@ -126,10 +143,10 @@
     stats[1] = jnp.zeros((QSETS + 1, 8, ROWS), jnp.float32)
     m_s[...] = jnp.full_like(m_s, LOW)
 
-    def body(i, carry):
+    def body(i, carry, masked):
         us = [table[T_QSET + i * PAIR_STEPS + k] for k in range(PAIR_STEPS)]
         js = [table[T_BLOCK + i * PAIR_STEPS + k] for k in range(PAIR_STEPS)]
-        scs = [masked_scores(table, kv[block_rows(j), 0:HEAD], q_t, u, j) for u, j in zip(us, js)]
+        scs = [masked_scores(table, kv[block_rows(j), 0:HEAD], q_t, u, j, masked) for u, j in zip(us, js)]
         tops = [jnp.max(sc, axis=0, keepdims=True) for sc in scs]
         for u, j, sc, top in zip(us, js, scs, tops):
             old = m_s[u]
@@ -144,7 +161,7 @@
             )
         return carry
 
-    lax.fori_loop(0, (table[T_COUNT] + PAIR_STEPS - 1) // PAIR_STEPS, body, 0)
+    step_loops(table, body)
     stats[0] = m_s[...]
 
 
@@ -195,10 +212,10 @@
     acc[...] = jnp.zeros_like(acc)
     dq_t[...] = jnp.zeros_like(dq_t)
 
-    def body(i, carry):
+    def body(i, carry, masked):
         us = [table[T_QSET + i * PAIR_STEPS + k] for k in range(PAIR_STEPS)]
         js = [table[T_BLOCK + i * PAIR_STEPS + k] for k in range(PAIR_STEPS)]
-        scs = [masked_scores(table, kv[block_rows(j), 0:HEAD], q_t, u, j) for u, j in zip(us, js)]
+        scs = [masked_scores(table, kv[block_rows(j), 0:HEAD], q_t, u, j, masked) for u, j in zip(us, js)]
         dps = [
             jnp.dot(kv[block_rows(j), HEAD:2 * HEAD], g_t[u], preferred_element_type=jnp.float32)
             for u, j in zip(us, js)
@@ -216,7 +233,7 @@
             )
         return carry
 
-    lax.fori_loop(0, (table[T_COUNT] + PAIR_STEPS - 1) // PAIR_STEPS, body, 0)
+    step_loops(table, body)
 
     for i in range(KEY_DEVICES):
         rank = table[T_RANK + i]
@@ -349,7 +366,8 @@
         project_own_kernel, "project_own", [((heads, rows), f32), ((NY - 1, heads, columns), bf16)],
         3 * 10**8, [out_grad, out_weight], [copies],
     )
-    all_queries = [queries] + [shift(queries, "x", k) for k in (1, 2, 3)]
+    near_queries = shift(queries, "x", 1)
+    all_queries = [queries, near_queries, shift(near_queries, "x", 1), shift(queries, "x", 3)]
     (summed,) = project_call(
         project_near_kernel, "project_near", [((heads, rows), f32)], 6 * 10**8,
         [parts[1], parts[3], rest, summed],
@@ -360,7 +378,8 @@
     )
 
     along_z = lax.all_to_all(copies, "z", 0, 0, tiled=True)
-    along_z = after(along_z, head_grads, all_queries[1], all_queries[3])
+    marks = sum(array[:8, :HEAD] for array in (head_grads, *all_queries[1:]))
+    along_z = after(along_z, marks)
     chunks = [along_z, shift(along_z, "c", 1)]
 
     kv, q_n, q_t, stats, o_t = kernel_call(

time: 111 us -> 99.3 us (0.89)
  Pallas kernels: 32.7 us -> 28.2 us
  local copies, waits for them, and re-layouts: 10.6 us -> 7.31 us
  starting transfers between devices: 41.4 us -> 38.6 us
  waiting for transfers between devices: 23 us -> 21.6 us
    pallas_call x3, Pallas kernels: 25.6 us -> 21 us  [kernel_call(): pl.pallas_call(body, out_shape=tuple((jax.ShapeDtypeStruct(s, d) for s, d...]
    ppermute x17, starting transfers between devices: 26.4 us -> 22.6 us  [shift(): lax.ppermute(value, axis, [(i, (i + distance) % size) for i in range(size)])]
    unnamed x26 -> x14, local copies, waits for them, and re-layouts: 9.83 us -> 6.58 us
    ppermute x17, waiting for transfers between devices: 17.9 us -> 16.4 us  [shift(): lax.ppermute(value, axis, [(i, (i + distance) % size) for i in range(size)])]
  transfers between devices with their start and end apart: 19 -> 19, of which waited for: 8 -> 9; matrix products, arithmetic and copies ran while one was open for 1% -> 1% of each run, Pallas kernels for 15% -> 14%
where the time goes in v3:
time: 99.3 us; the launch traced here: 98.9 us
  starting transfers between devices  38.6 us (39%)
  Pallas kernels  28.2 us (28%)
  waiting for transfers between devices  21.6 us (22%)
  local copies, waits for them, and re-layouts  7.31 us (7%)
  other arithmetic  2.43 us (2%)
    ppermute x17, starting transfers between devices, shift(): lax.ppermute(value, axis, [(i, (i + distance) % size) for i in range(size)])  22.6 us
    pallas_call x3, Pallas kernels, kernel_call(): pl.pallas_call(body, out_shape=tuple((jax.ShapeDtypeStruct(s, d) for s, d...  21 us
    ppermute x17, waiting for transfers between devices, shift(): lax.ppermute(value, axis, [(i, (i + distance) % size) for i in range(size)])  16.4 us
    all_to_all x1, starting transfers between devices, shards(): along_z = lax.all_to_all(copies, 'z', 0, 0, tiled=True)  9.01 us
    all_to_all x1, starting transfers between devices, shards(): total = lax.all_to_all(total.astype(bf16), 'z', 0, 0, tiled=True)  6.95 us
    unnamed x14, local copies, waits for them, and re-layouts  6.58 us
    all_to_all x1, waiting for transfers between devices, shards(): total = lax.all_to_all(total.astype(bf16), 'z', 0, 0, tiled=True)  5.19 us
    pallas_call x3, Pallas kernels, project_call(): pl.pallas_call(body, out_shape=tuple((jax.ShapeDtypeStruct(s, d) for s, d...  3.42 us
  transfers between devices with their start and end apart: 19, of which 9 were waited for; matrix products, arithmetic and copies ran while one was open for 1% of the time, Pallas kernels for 14%

profile of v3, /device:TPU:1, one launch (start us, length us, event | category | flops | bytes accessed | tf_op | source)
XLA Modules:
  0.0 98.9 jit_solution(10496889053497120729)
XLA Ops:
  0.6 0.0 copy-start.4
  0.6 0.0 copy-start.6
  0.7 1.7 %spread.1.unread = bf16[8,128,256]{2,1,0:T(8,128)(2,1)} custom-call(bf16[128,128]{1,0:T(8,128)(2,1)} %keys.1, bf16[128,128]{1,0:T(8,128)(2,1)} %values.1), custom_call_target="tpu_custom_call" | custom-call | flops 20000000000 | bytes 1000000 | tf_op jit(solution)/shard_map/spread/pallas_call | solution.py:355
  2.4 9.0 %all-to-all-start = ((bf16[8,128,256]{2,1,0:T(8,128)(2,1)}), bf16[8,128,256]{2,1,0:T(8,128)(2,1)S(1)}, u32[]{:S(2)}, u32[]{:S(2)}) async-start(bf16[8,128,256]{2,1,0:T(8,128)(2,1)} %spread.1.unread), calls=%async_computation | async-start | bytes 1048576 | tf_op jit(solution)/shard_map/all_to_all | solution.py:380
  11.4 0.0 copy-done.4
  11.4 1.4 %collective-permute-start.1 = (bf16[128,1536]{1,0:T(8,128)(2,1)S(1)}, bf16[128,1536]{1,0:T(8,128)(2,1)S(1)}, u32[]{:S(2)}, u32[]{:S(2)}) collective-permute-start(bf16[128,1536]{1,0:T(8,128)(2,1)S(1)} %copy-done.4), channel_id=1, source_target_pairs={{0,1},{1,2},{2,3},{3,0},{4,5},{5,6},{6,7},{7,4},{8,9},{9,10},{10,1... | collective-permute-start | bytes 1179656 | tf_op jit(solution)/shard_map/ppermute | solution.py:343
  12.8 1.5 %collective-permute-start.2 = (bf16[128,1536]{1,0:T(8,128)(2,1)S(1)}, bf16[128,1536]{1,0:T(8,128)(2,1)S(1)}, u32[]{:S(2)}, u32[]{:S(2)}) collective-permute-start(bf16[128,1536]{1,0:T(8,128)(2,1)S(1)} %copy-done.4), channel_id=1, source_target_pairs={{0,3},{1,0},{2,1},{3,2},{4,7},{5,4},{6,5},{7,6},{8,11},{9,8},{10,9... | collective-permute-start | bytes 1179656 | tf_op jit(solution)/shard_map/ppermute | solution.py:343
  14.3 1.6 %collective-permute-start = (bf16[128,1536]{1,0:T(8,128)(2,1)S(1)}, bf16[128,1536]{1,0:T(8,128)(2,1)S(1)}, u32[]{:S(2)}, u32[]{:S(2)}) collective-permute-start(bf16[128,1536]{1,0:T(8,128)(2,1)S(1)} %copy-done.4), channel_id=1, source_target_pairs={{0,2},{1,3},{2,0},{3,1},{4,6},{5,7},{6,4},{7,5},{8,10},{9,11},{10,... | collective-permute-start | bytes 1179656 | tf_op jit(solution)/shard_map/ppermute | solution.py:343
  15.8 0.0 copy-done.6
  15.8 1.2 %collective-permute-start.6 = (bf16[128,768]{1,0:T(8,128)(2,1)S(1)}, bf16[128,768]{1,0:T(8,128)(2,1)S(1)}, u32[]{:S(2)}, u32[]{:S(2)}) collective-permute-start(bf16[128,768]{1,0:T(8,128)(2,1)S(1)} %copy-done.6), channel_id=1, source_target_pairs={{0,8},{8,16},{16,24},{24,0},{1,9},{9,17},{17,25},{25,1},{2,10},{10... | collective-permute-start | bytes 589832 | tf_op jit(solution)/shard_map/ppermute | solution.py:343
  17.1 1.5 %collective-permute-start.8 = (bf16[128,768]{1,0:T(8,128)(2,1)S(1)}, bf16[128,768]{1,0:T(8,128)(2,1)S(1)}, u32[]{:S(2)}, u32[]{:S(2)}) collective-permute-start(bf16[128,768]{1,0:T(8,128)(2,1)S(1)} %copy-done.6), channel_id=1, source_target_pairs={{0,24},{8,0},{16,8},{24,16},{1,25},{9,1},{17,9},{25,17},{2,26},{10... | collective-permute-start | bytes 589832 | tf_op jit(solution)/shard_map/ppermute | solution.py:343
  18.5 3.3 %collective-permute-done.6.refs_1_ = bf16[128,768]{1,0:T(8,128)(2,1)S(1)} collective-permute-done((bf16[128,768]{1,0:T(8,128)(2,1)S(1)}, bf16[128,768]{1,0:T(8,128)(2,1)S(1)}, u32[]{:S(2)}, u32[]{:S(2)}) %collective-permute-start.6) | collective-permute-done | bytes 196640 | tf_op jit(solution)/shard_map/ppermute | solution.py:343
  21.9 0.0 collective-permute-start.7
  21.9 2.0 %tables.1.refs_0_.table = s32[192]{0:T(256)} custom-call(s32[64]{0:T(128)} %pair.1), custom_call_target="tpu_custom_call" | custom-call | flops 1000000 | bytes 1000 | tf_op jit(solution)/shard_map/tables/pallas_call | solution.py:85
  23.9 0.0 copy-start
  23.9 3.7 %copy-done = bf16[768,6144]{1,0:T(8,128)(2,1)S(1)} copy-done((bf16[768,6144]{1,0:T(8,128)(2,1)S(1)}, bf16[768,6144]{1,0:T(8,128)(2,1)}, u32[]{:S(2)}) %copy-start) | copy-done | bytes 9437208
  27.6 0.0 copy-start.1
  27.6 1.0 %copy-done.1 = bf16[8,128,256]{2,1,0:T(8,128)(2,1)S(1)} copy-done((bf16[8,128,256]{2,1,0:T(8,128)(2,1)S(1)}, bf16[8,128,256]{2,1,0:T(8,128)(2,1)}, u32[]{:S(2)}) %copy-start.1) | copy-done | bytes 524312
  28.6 0.0 copy-start.5
  28.6 1.2 %project_own.1 = (f32[768,128]{1,0:T(8,128)S(1)}, bf16[3,768,1536]{2,1,0:T(8,128)(2,1)S(1)}) custom-call(bf16[128,1536]{1,0:T(8,128)(2,1)S(1)} %copy-done.4, bf16[768,6144]{1,0:T(8,128)(2,1)S(1)} %copy-done, bf16[8,128,256]{2,1,0:T(8,128)(2,1)S(1)} %copy-done.1), custom_call_target="tpu_custom_call" | custom-call | flops 300000000 | bytes 1000000 | tf_op jit(solution)/shard_map/project_own/pallas_call | solution.py:291
  29.8 0.0 collective-permute-done.1.one
  29.8 0.0 collective-permute-done.2.three
  29.9 1.4 %project_near.1.sum_ref = f32[768,128]{1,0:T(8,128)S(1)} custom-call(bf16[128,1536]{1,0:T(8,128)(2,1)S(1)} %collective-permute-done.1.one, bf16[128,1536]{1,0:T(8,128)(2,1)S(1)} %collective-permute-done.2.three, bf16[3,768,1536]{2,1,0:T(8,128)(2,1)S(1)} %get-tuple-element.16.rest, f32[768,128]{1,0:T(8,128)S(1)} %get-tuple-element.17.sum_ref), custom_call_target="tpu_custom_call" | custom-call | flops 600000000 | bytes 1000000 | tf_op jit(solution)/shard_map/project_near/pallas_call | solution.py:291
  31.2 0.8 collective-permute-done.part
  32.0 0.0 copy-done.5
  32.0 0.8 project_far.1.refs_0_
  32.9 0.0 collective-permute-done.8.refs_3_
  32.9 0.0 collective-permute-done.7.refs_2_
  32.9 0.6 slice_add_fusion.refs_1_
  33.5 0.0 all-to-all-done.refs_0_
  33.5 0.0 copy-start.2
  33.5 0.8 copy-done.2
  34.3 2.2 %collective-permute-start.9 = (bf16[8,128,256]{2,1,0:T(8,128)(2,1)}, bf16[8,128,256]{2,1,0:T(8,128)(2,1)S(1)}, u32[]{:S(2)}, u32[]{:S(2)}) collective-permute-start(bf16[8,128,256]{2,1,0:T(8,128)(2,1)} %after.1.refs_4_), channel_id=1, source_target_pairs={{0,4},{4,0},{1,5},{5,1},{2,6},{6,2},{3,7},{7,3},{8,12},{12,8},{9,1... | collective-permute-start | bytes 1572872 | tf_op jit(solution)/shard_map/ppermute | solution.py:343
  36.5 1.2 %collective-permute-start.3 = (bf16[128,768]{1,0:T(8,128)(2,1)S(1)}, bf16[128,768]{1,0:T(8,128)(2,1)S(1)}, u32[]{:S(2)}, u32[]{:S(2)}) collective-permute-start(bf16[128,768]{1,0:T(8,128)(2,1)S(1)} %project_far.1.refs_0_), channel_id=1, source_target_pairs={{0,8},{8,16},{16,24},{24,0},{1,9},{9,17},{17,25},{25,1},{2,10},{10... | collective-permute-start | bytes 589832 | tf_op jit(solution)/shard_map/ppermute | solution.py:343
  37.7 2.6 %collective-permute-start.4 = (bf16[128,768]{1,0:T(8,128)(2,1)S(1)}, bf16[128,768]{1,0:T(8,128)(2,1)S(1)}, u32[]{:S(2)}, u32[]{:S(2)}) collective-permute-start(bf16[128,768]{1,0:T(8,128)(2,1)S(1)} %project_far.1.refs_0_), channel_id=1, source_target_pairs={{0,16},{8,24},{16,0},{24,8},{1,17},{9,25},{17,1},{25,9},{2,18},{10... | collective-permute-start | bytes 589832 | tf_op jit(solution)/shard_map/ppermute | solution.py:343
  40.3 0.7 collective-permute-start.5
  41.0 0.0 collective-permute-done.9.refs_5_
  41.0 1.0 %copy-done.3 = bf16[8,128,256]{2,1,0:T(8,128)(2,1)S(1)} copy-done((bf16[8,128,256]{2,1,0:T(8,128)(2,1)S(1)}, bf16[8,128,256]{2,1,0:T(8,128)(2,1)}, u32[]{:S(2)}) %copy-start.3) | copy-done | bytes 524312
  42.0 8.3 %forward.1 = (bf16[2048,256]{1,0:T(8,128)(2,1)S(1)}, bf16[9,384,128]{2,1,0:T(8,128)(2,1)S(1)}, bf16[9,128,384]{2,1,0:T(8,128)(2,1)S(1)}, f32[2,9,8,384]{3,2,1,0:T(8,128)S(1)}, f32[9,128,384]{2,1,0:T(8,128)S(1)}) custom-call(s32[192]{0:T(256)S(1)} %copy-done.5, bf16[128,768]{1,0:T(8,128)(2,1)S(1)} %copy-done.6, ...), custom_call_target="tpu_custom_call" | custom-call | flops 4000000000 | bytes 1000000 | tf_op jit(solution)/shard_map/forward/pallas_call | solution.py:307
  50.3 0.0 collective-permute-done.3.refs_1_
  50.3 0.0 collective-permute-done.4.refs_2_
  50.3 0.0 collective-permute-done.5.refs_3_
  50.3 0.9 weights.1
  51.3 0.8 collective-permute-start.10
  52.1 1.8 %collective-permute-start.11 = (f32[3,8,384]{2,1,0:T(8,128)S(1)}, f32[3,8,384]{2,1,0:T(8,128)S(1)}, u32[]{:S(2)}, u32[]{:S(2)}) collective-permute-start(f32[3,8,384]{2,1,0:T(8,128)S(1)} %get-tuple-element.20.refs_0_), channel_id=1, source_target_pairs={{0,16},{8,24},{16,0},{24,8},{1,17},{9,25},{17,1},{25,9},{2,18},{10... | collective-permute-start | bytes 110600 | tf_op jit(solution)/shard_map/ppermute | solution.py:343
  53.9 0.7 collective-permute-start.12
  54.6 0.8 collective-permute-done.10.refs_1_
  55.4 1.3 %collective-permute-done.11.refs_2_ = f32[3,8,384]{2,1,0:T(8,128)S(1)} collective-permute-done((f32[3,8,384]{2,1,0:T(8,128)S(1)}, f32[3,8,384]{2,1,0:T(8,128)S(1)}, u32[]{:S(2)}, u32[]{:S(2)}) %collective-permute-start.11) | collective-permute-done | bytes 36896 | tf_op jit(solution)/shard_map/ppermute | solution.py:343
  56.7 0.3 collective-permute-done.12.refs_3_
  57.0 11.9 %backward.1 = (f32[128,768]{1,0:T(8,128)S(1)}, bf16[3,128,768]{2,1,0:T(8,128)(2,1)S(1)}, bf16[16,128,256]{2,1,0:T(8,128)(2,1)S(1)}) custom-call(s32[192]{0:T(256)S(1)} %copy-done.5, f32[3,8,384]{2,1,0:T(8,128)S(1)} %get-tuple-element.20.refs_0_, f32[3,8,384]{2,1,0:T(8,128)S(1)} %collective-permute-done.10.refs_1_, ...), custom_call_target="tpu_custom_call" | custom-call | flops 8000000000 | bytes 1000000 | tf_op jit(solution)/shard_map/backward/pallas_call | solution.py:307
  68.9 1.9 %collective-permute-start.16 = (bf16[8,128,256]{2,1,0:T(8,128)(2,1)S(1)}, bf16[8,128,256]{2,1,0:T(8,128)(2,1)S(1)}, u32[]{:S(2)}, u32[]{:S(2)}) collective-permute-start(bf16[8,128,256]{2,1,0:T(8,128)(2,1)S(1)} %slice.43), channel_id=1, source_target_pairs={{0,4},{4,0},{1,5},{5,1},{2,6},{6,2},{3,7},{7,3},{8,12},{12,8},{9,1... | collective-permute-start | bytes 1572872 | tf_op jit(solution)/shard_map/ppermute | solution.py:343
  70.8 1.5 %collective-permute-done.16 = bf16[8,128,256]{2,1,0:T(8,128)(2,1)S(1)} collective-permute-done((bf16[8,128,256]{2,1,0:T(8,128)(2,1)S(1)}, bf16[8,128,256]{2,1,0:T(8,128)(2,1)S(1)}, u32[]{:S(2)}, u32[]{:S(2)}) %collective-permute-start.16) | collective-permute-done | bytes 524320 | tf_op jit(solution)/shard_map/ppermute | solution.py:343
  72.3 0.9 add_convert_fusion
  73.3 6.9 %all-to-all-start.1 = ((bf16[8,128,256]{2,1,0:T(8,128)(2,1)}), bf16[8,128,256]{2,1,0:T(8,128)(2,1)S(1)}, u32[]{:S(2)}, u32[]{:S(2)}) async-start(bf16[8,128,256]{2,1,0:T(8,128)(2,1)} %add_convert_fusion), calls=%async_computation.1 | async-start | bytes 1048576 | tf_op jit(solution)/shard_map/all_to_all | solution.py:413
  80.3 1.1 %collective-permute-start.13 = (bf16[128,768]{1,0:T(8,128)(2,1)S(1)}, bf16[128,768]{1,0:T(8,128)(2,1)S(1)}, u32[]{:S(2)}, u32[]{:S(2)}) collective-permute-start(bf16[128,768]{1,0:T(8,128)(2,1)S(1)} %get-tuple-element.29), channel_id=1, source_target_pairs={{0,8},{8,16},{16,24},{24,0},{1,9},{9,17},{17,25},{25,1},{2,10},{10... | collective-permute-start | bytes 589832 | tf_op jit(solution)/shard_map/ppermute | solution.py:343
  81.3 2.3 %collective-permute-start.14 = (bf16[128,768]{1,0:T(8,128)(2,1)S(1)}, bf16[128,768]{1,0:T(8,128)(2,1)S(1)}, u32[]{:S(2)}, u32[]{:S(2)}) collective-permute-start(bf16[128,768]{1,0:T(8,128)(2,1)S(1)} %get-tuple-element.31), channel_id=1, source_target_pairs={{0,16},{8,24},{16,0},{24,8},{1,17},{9,25},{17,1},{25,9},{2,18},{10... | collective-permute-start | bytes 589832 | tf_op jit(solution)/shard_map/ppermute | solution.py:343
  83.6 0.2 collective-permute-start.15
  83.8 3.5 %collective-permute-done.13 = bf16[128,768]{1,0:T(8,128)(2,1)S(1)} collective-permute-done((bf16[128,768]{1,0:T(8,128)(2,1)S(1)}, bf16[128,768]{1,0:T(8,128)(2,1)S(1)}, u32[]{:S(2)}, u32[]{:S(2)}) %collective-permute-start.13) | collective-permute-done | bytes 196640 | tf_op jit(solution)/shard_map/ppermute | solution.py:343
  87.3 4.8 %collective-permute-done.14 = bf16[128,768]{1,0:T(8,128)(2,1)S(1)} collective-permute-done((bf16[128,768]{1,0:T(8,128)(2,1)S(1)}, bf16[128,768]{1,0:T(8,128)(2,1)S(1)}, u32[]{:S(2)}, u32[]{:S(2)}) %collective-permute-start.14) | collective-permute-done | bytes 196640 | tf_op jit(solution)/shard_map/ppermute | solution.py:343
  92.2 0.0 collective-permute-done.15
  92.2 0.8 convert_add_fusion
  93.0 5.2 %all-to-all-done.1 = bf16[8,128,256]{2,1,0:T(8,128)(2,1)S(1)} async-done(((bf16[8,128,256]{2,1,0:T(8,128)(2,1)}), bf16[8,128,256]{2,1,0:T(8,128)(2,1)S(1)}, u32[]{:S(2)}, u32[]{:S(2)}) %all-to-all-start.1) | async-done | bytes 524320 | tf_op jit(solution)/shard_map/all_to_all | solution.py:413
  98.2 0.1 convert_reduce_fusion
  98.2 0.7 fusion
  (4 shorter events, 0.1 us)
Async XLA Ops:
  0.6 10.8 %copy-start.4 = (bf16[128,1536]{1,0:T(8,128)(2,1)S(1)}, bf16[128,1536]{1,0:T(8,128)(2,1)}, u32[]{:S(2)}) copy-start(bf16[128,1536]{1,0:T(8,128)(2,1)} %own.1) | copy-start | bytes 1179652
  0.6 15.2 %copy-start.6 = (bf16[128,768]{1,0:T(8,128)(2,1)S(1)}, bf16[128,768]{1,0:T(8,128)(2,1)}, u32[]{:S(2)}) copy-start(bf16[128,768]{1,0:T(8,128)(2,1)} %refs_0_.1) | copy-start | bytes 589828
  2.4 31.1 %all-to-all-start = ((bf16[8,128,256]{2,1,0:T(8,128)(2,1)}), bf16[8,128,256]{2,1,0:T(8,128)(2,1)S(1)}, u32[]{:S(2)}, u32[]{:S(2)}) async-start(bf16[8,128,256]{2,1,0:T(8,128)(2,1)} %spread.1.unread), calls=%async_computation | async-start | bytes 1048576 | tf_op jit(solution)/shard_map/all_to_all | solution.py:380
  11.4 18.5 %collective-permute-start.1 = (bf16[128,1536]{1,0:T(8,128)(2,1)S(1)}, bf16[128,1536]{1,0:T(8,128)(2,1)S(1)}, u32[]{:S(2)}, u32[]{:S(2)}) collective-permute-start(bf16[128,1536]{1,0:T(8,128)(2,1)S(1)} %copy-done.4), channel_id=1, source_target_pairs={{0,1},{1,2},{2,3},{3,0},{4,5},{5,6},{6,7},{7,4},{8,9},{9,10},{10,1... | collective-permute-start | bytes 1179656 | tf_op jit(solution)/shard_map/ppermute | solution.py:343
  12.8 17.1 %collective-permute-start.2 = (bf16[128,1536]{1,0:T(8,128)(2,1)S(1)}, bf16[128,1536]{1,0:T(8,128)(2,1)S(1)}, u32[]{:S(2)}, u32[]{:S(2)}) collective-permute-start(bf16[128,1536]{1,0:T(8,128)(2,1)S(1)} %copy-done.4), channel_id=1, source_target_pairs={{0,3},{1,0},{2,1},{3,2},{4,7},{5,4},{6,5},{7,6},{8,11},{9,8},{10,9... | collective-permute-start | bytes 1179656 | tf_op jit(solution)/shard_map/ppermute | solution.py:343
  14.3 17.7 %collective-permute-start = (bf16[128,1536]{1,0:T(8,128)(2,1)S(1)}, bf16[128,1536]{1,0:T(8,128)(2,1)S(1)}, u32[]{:S(2)}, u32[]{:S(2)}) collective-permute-start(bf16[128,1536]{1,0:T(8,128)(2,1)S(1)} %copy-done.4), channel_id=1, source_target_pairs={{0,2},{1,3},{2,0},{3,1},{4,6},{5,7},{6,4},{7,5},{8,10},{9,11},{10,... | collective-permute-start | bytes 1179656 | tf_op jit(solution)/shard_map/ppermute | solution.py:343
  15.8 6.0 %collective-permute-start.6 = (bf16[128,768]{1,0:T(8,128)(2,1)S(1)}, bf16[128,768]{1,0:T(8,128)(2,1)S(1)}, u32[]{:S(2)}, u32[]{:S(2)}) collective-permute-start(bf16[128,768]{1,0:T(8,128)(2,1)S(1)} %copy-done.6), channel_id=1, source_target_pairs={{0,8},{8,16},{16,24},{24,0},{1,9},{9,17},{17,25},{25,1},{2,10},{10... | collective-permute-start | bytes 589832 | tf_op jit(solution)/shard_map/ppermute | solution.py:343
  17.1 15.8 %collective-permute-start.8 = (bf16[128,768]{1,0:T(8,128)(2,1)S(1)}, bf16[128,768]{1,0:T(8,128)(2,1)S(1)}, u32[]{:S(2)}, u32[]{:S(2)}) collective-permute-start(bf16[128,768]{1,0:T(8,128)(2,1)S(1)} %copy-done.6), channel_id=1, source_target_pairs={{0,24},{8,0},{16,8},{24,16},{1,25},{9,1},{17,9},{25,17},{2,26},{10... | collective-permute-start | bytes 589832 | tf_op jit(solution)/shard_map/ppermute | solution.py:343
  21.9 11.0 %collective-permute-start.7 = (bf16[128,768]{1,0:T(8,128)(2,1)S(1)}, bf16[128,768]{1,0:T(8,128)(2,1)S(1)}, u32[]{:S(2)}, u32[]{:S(2)}) collective-permute-start(bf16[128,768]{1,0:T(8,128)(2,1)S(1)} %collective-permute-done.6.refs_1_), channel_id=1, source_target_pairs={{0,8},{8,16},{16,24},{24,0},{1,9},{9,17},{17,25},{25,1},{2,10},{10... | collective-permute-start | bytes 589832 | tf_op jit(solution)/shard_map/ppermute | solution.py:343
  23.9 3.7 %copy-start = (bf16[768,6144]{1,0:T(8,128)(2,1)S(1)}, bf16[768,6144]{1,0:T(8,128)(2,1)}, u32[]{:S(2)}) copy-start(bf16[768,6144]{1,0:T(8,128)(2,1)} %w_ref.1) | copy-start | bytes 28311556
  27.6 1.0 %copy-start.1 = (bf16[8,128,256]{2,1,0:T(8,128)(2,1)S(1)}, bf16[8,128,256]{2,1,0:T(8,128)(2,1)}, u32[]{:S(2)}) copy-start(bf16[8,128,256]{2,1,0:T(8,128)(2,1)} %spread.1.unread) | copy-start | bytes 1572868
  28.6 3.4 %copy-start.5 = (s32[192]{0:T(256)S(1)}, s32[192]{0:T(256)}, u32[]{:S(2)}) copy-start(s32[192]{0:T(256)} %tables.1.refs_0_.table) | copy-start | bytes 2308
  33.5 0.8 copy-start.2
  34.3 6.7 %collective-permute-start.9 = (bf16[8,128,256]{2,1,0:T(8,128)(2,1)}, bf16[8,128,256]{2,1,0:T(8,128)(2,1)S(1)}, u32[]{:S(2)}, u32[]{:S(2)}) collective-permute-start(bf16[8,128,256]{2,1,0:T(8,128)(2,1)} %after.1.refs_4_), channel_id=1, source_target_pairs={{0,4},{4,0},{1,5},{5,1},{2,6},{6,2},{3,7},{7,3},{8,12},{12,8},{9,1... | collective-permute-start | bytes 1572872 | tf_op jit(solution)/shard_map/ppermute | solution.py:343
  36.5 13.9 %collective-permute-start.3 = (bf16[128,768]{1,0:T(8,128)(2,1)S(1)}, bf16[128,768]{1,0:T(8,128)(2,1)S(1)}, u32[]{:S(2)}, u32[]{:S(2)}) collective-permute-start(bf16[128,768]{1,0:T(8,128)(2,1)S(1)} %project_far.1.refs_0_), channel_id=1, source_target_pairs={{0,8},{8,16},{16,24},{24,0},{1,9},{9,17},{17,25},{25,1},{2,10},{10... | collective-permute-start | bytes 589832 | tf_op jit(solution)/shard_map/ppermute | solution.py:343
  37.7 12.6 %collective-permute-start.4 = (bf16[128,768]{1,0:T(8,128)(2,1)S(1)}, bf16[128,768]{1,0:T(8,128)(2,1)S(1)}, u32[]{:S(2)}, u32[]{:S(2)}) collective-permute-start(bf16[128,768]{1,0:T(8,128)(2,1)S(1)} %project_far.1.refs_0_), channel_id=1, source_target_pairs={{0,16},{8,24},{16,0},{24,8},{1,17},{9,25},{17,1},{25,9},{2,18},{10... | collective-permute-start | bytes 589832 | tf_op jit(solution)/shard_map/ppermute | solution.py:343
  40.3 10.0 %collective-permute-start.5 = (bf16[128,768]{1,0:T(8,128)(2,1)S(1)}, bf16[128,768]{1,0:T(8,128)(2,1)S(1)}, u32[]{:S(2)}, u32[]{:S(2)}) collective-permute-start(bf16[128,768]{1,0:T(8,128)(2,1)S(1)} %project_far.1.refs_0_), channel_id=1, source_target_pairs={{0,24},{8,0},{16,8},{24,16},{1,25},{9,1},{17,9},{25,17},{2,26},{10... | collective-permute-start | bytes 589832 | tf_op jit(solution)/shard_map/ppermute | solution.py:343
  41.0 1.0 %copy-start.3 = (bf16[8,128,256]{2,1,0:T(8,128)(2,1)S(1)}, bf16[8,128,256]{2,1,0:T(8,128)(2,1)}, u32[]{:S(2)}) copy-start(bf16[8,128,256]{2,1,0:T(8,128)(2,1)} %after.1.refs_4_) | copy-start | bytes 1572868
  51.3 4.1 %collective-permute-start.10 = (f32[3,8,384]{2,1,0:T(8,128)S(1)}, f32[3,8,384]{2,1,0:T(8,128)S(1)}, u32[]{:S(2)}, u32[]{:S(2)}) collective-permute-start(f32[3,8,384]{2,1,0:T(8,128)S(1)} %get-tuple-element.20.refs_0_), channel_id=1, source_target_pairs={{0,8},{8,16},{16,24},{24,0},{1,9},{9,17},{17,25},{25,1},{2,10},{10... | collective-permute-start | bytes 110600 | tf_op jit(solution)/shard_map/ppermute | solution.py:343
  52.1 4.6 %collective-permute-start.11 = (f32[3,8,384]{2,1,0:T(8,128)S(1)}, f32[3,8,384]{2,1,0:T(8,128)S(1)}, u32[]{:S(2)}, u32[]{:S(2)}) collective-permute-start(f32[3,8,384]{2,1,0:T(8,128)S(1)} %get-tuple-element.20.refs_0_), channel_id=1, source_target_pairs={{0,16},{8,24},{16,0},{24,8},{1,17},{9,25},{17,1},{25,9},{2,18},{10... | collective-permute-start | bytes 110600 | tf_op jit(solution)/shard_map/ppermute | solution.py:343
  53.9 3.1 %collective-permute-start.12 = (f32[3,8,384]{2,1,0:T(8,128)S(1)}, f32[3,8,384]{2,1,0:T(8,128)S(1)}, u32[]{:S(2)}, u32[]{:S(2)}) collective-permute-start(f32[3,8,384]{2,1,0:T(8,128)S(1)} %get-tuple-element.20.refs_0_), channel_id=1, source_target_pairs={{0,24},{8,0},{16,8},{24,16},{1,25},{9,1},{17,9},{25,17},{2,26},{10... | collective-permute-start | bytes 110600 | tf_op jit(solution)/shard_map/ppermute | solution.py:343
  68.9 3.4 %collective-permute-start.16 = (bf16[8,128,256]{2,1,0:T(8,128)(2,1)S(1)}, bf16[8,128,256]{2,1,0:T(8,128)(2,1)S(1)}, u32[]{:S(2)}, u32[]{:S(2)}) collective-permute-start(bf16[8,128,256]{2,1,0:T(8,128)(2,1)S(1)} %slice.43), channel_id=1, source_target_pairs={{0,4},{4,0},{1,5},{5,1},{2,6},{6,2},{3,7},{7,3},{8,12},{12,8},{9,1... | collective-permute-start | bytes 1572872 | tf_op jit(solution)/shard_map/ppermute | solution.py:343
  73.3 24.9 %all-to-all-start.1 = ((bf16[8,128,256]{2,1,0:T(8,128)(2,1)}), bf16[8,128,256]{2,1,0:T(8,128)(2,1)S(1)}, u32[]{:S(2)}, u32[]{:S(2)}) async-start(bf16[8,128,256]{2,1,0:T(8,128)(2,1)} %add_convert_fusion), calls=%async_computation.1 | async-start | bytes 1048576 | tf_op jit(solution)/shard_map/all_to_all | solution.py:413
  80.3 7.1 %collective-permute-start.13 = (bf16[128,768]{1,0:T(8,128)(2,1)S(1)}, bf16[128,768]{1,0:T(8,128)(2,1)S(1)}, u32[]{:S(2)}, u32[]{:S(2)}) collective-permute-start(bf16[128,768]{1,0:T(8,128)(2,1)S(1)} %get-tuple-element.29), channel_id=1, source_target_pairs={{0,8},{8,16},{16,24},{24,0},{1,9},{9,17},{17,25},{25,1},{2,10},{10... | collective-permute-start | bytes 589832 | tf_op jit(solution)/shard_map/ppermute | solution.py:343
  81.3 10.8 %collective-permute-start.14 = (bf16[128,768]{1,0:T(8,128)(2,1)S(1)}, bf16[128,768]{1,0:T(8,128)(2,1)S(1)}, u32[]{:S(2)}, u32[]{:S(2)}) collective-permute-start(bf16[128,768]{1,0:T(8,128)(2,1)S(1)} %get-tuple-element.31), channel_id=1, source_target_pairs={{0,16},{8,24},{16,0},{24,8},{1,17},{9,25},{17,1},{25,9},{2,18},{10... | collective-permute-start | bytes 589832 | tf_op jit(solution)/shard_map/ppermute | solution.py:343
  83.6 8.5 %collective-permute-start.15 = (bf16[128,768]{1,0:T(8,128)(2,1)S(1)}, bf16[128,768]{1,0:T(8,128)(2,1)S(1)}, u32[]{:S(2)}, u32[]{:S(2)}) collective-permute-start(bf16[128,768]{1,0:T(8,128)(2,1)S(1)} %get-tuple-element.30), channel_id=1, source_target_pairs={{0,24},{8,0},{16,8},{24,16},{1,25},{9,1},{17,9},{25,17},{2,26},{10... | collective-permute-start | bytes 589832 | tf_op jit(solution)/shard_map/ppermute | solution.py:343

commit v4 on v3

--- a/solution.py
+++ b/solution.py
@@ -26,7 +26,7 @@
 TABLE = 192
 SPREAD_FLOPS = 2 * 10**10
 LOW = -1e30
-PAIR_STEPS = 4
+PAIR_STEPS = 6
 
 
 def table_kernel(pair, table):

time: 99.3 us -> 98.8 us (level)
  Pallas kernels: 28.2 us -> 27.2 us
  transfers between devices with their start and end apart: 19 -> 19, of which waited for: 9 -> 9; matrix products, arithmetic and copies ran while one was open for 1% -> 1% of each run, Pallas kernels for 14% -> 13%
where the time goes in v4:
time: 98.8 us; the launch traced here: 98.4 us
  starting transfers between devices  38.6 us (39%)
  Pallas kernels  27.2 us (28%)
  waiting for transfers between devices  22.1 us (22%)
  local copies, waits for them, and re-layouts  7.31 us (7%)
  other arithmetic  2.43 us (2%)
    ppermute x17, starting transfers between devices, shift(): lax.ppermute(value, axis, [(i, (i + distance) % size) for i in range(size)])  22.8 us
    pallas_call x3, Pallas kernels, kernel_call(): pl.pallas_call(body, out_shape=tuple((jax.ShapeDtypeStruct(s, d) for s, d...  20.1 us
    ppermute x17, waiting for transfers between devices, shift(): lax.ppermute(value, axis, [(i, (i + distance) % size) for i in range(size)])  17 us
    all_to_all x1, starting transfers between devices, shards(): along_z = lax.all_to_all(copies, 'z', 0, 0, tiled=True)  9.01 us
    all_to_all x1, starting transfers between devices, shards(): total = lax.all_to_all(total.astype(bf16), 'z', 0, 0, tiled=True)  6.83 us
    unnamed x14, local copies, waits for them, and re-layouts  6.58 us
    all_to_all x1, waiting for transfers between devices, shards(): total = lax.all_to_all(total.astype(bf16), 'z', 0, 0, tiled=True)  5.06 us
    pallas_call x3, Pallas kernels, project_call(): pl.pallas_call(body, out_shape=tuple((jax.ShapeDtypeStruct(s, d) for s, d...  3.42 us
  transfers between devices with their start and end apart: 19, of which 9 were waited for; matrix products, arithmetic and copies ran while one was open for 1% of the time, Pallas kernels for 13%

profile of v4, /device:TPU:1, one launch (start us, length us, event | category | flops | bytes accessed | tf_op | source)
XLA Modules:
  0.0 98.4 jit_solution(780393583010921742)
XLA Ops:
  0.6 0.0 copy-start.4
  0.6 0.0 copy-start.6
  0.7 1.7 %spread.1.unread = bf16[8,128,256]{2,1,0:T(8,128)(2,1)} custom-call(bf16[128,128]{1,0:T(8,128)(2,1)} %keys.1, bf16[128,128]{1,0:T(8,128)(2,1)} %values.1), custom_call_target="tpu_custom_call" | custom-call | flops 20000000000 | bytes 1000000 | tf_op jit(solution)/shard_map/spread/pallas_call | solution.py:355
  2.4 9.0 %all-to-all-start = ((bf16[8,128,256]{2,1,0:T(8,128)(2,1)}), bf16[8,128,256]{2,1,0:T(8,128)(2,1)S(1)}, u32[]{:S(2)}, u32[]{:S(2)}) async-start(bf16[8,128,256]{2,1,0:T(8,128)(2,1)} %spread.1.unread), calls=%async_computation | async-start | bytes 1048576 | tf_op jit(solution)/shard_map/all_to_all | solution.py:380
  11.4 0.0 copy-done.4
  11.4 1.4 %collective-permute-start.1 = (bf16[128,1536]{1,0:T(8,128)(2,1)S(1)}, bf16[128,1536]{1,0:T(8,128)(2,1)S(1)}, u32[]{:S(2)}, u32[]{:S(2)}) collective-permute-start(bf16[128,1536]{1,0:T(8,128)(2,1)S(1)} %copy-done.4), channel_id=1, source_target_pairs={{0,1},{1,2},{2,3},{3,0},{4,5},{5,6},{6,7},{7,4},{8,9},{9,10},{10,1... | collective-permute-start | bytes 1179656 | tf_op jit(solution)/shard_map/ppermute | solution.py:343
  12.8 1.5 %collective-permute-start.2 = (bf16[128,1536]{1,0:T(8,128)(2,1)S(1)}, bf16[128,1536]{1,0:T(8,128)(2,1)S(1)}, u32[]{:S(2)}, u32[]{:S(2)}) collective-permute-start(bf16[128,1536]{1,0:T(8,128)(2,1)S(1)} %copy-done.4), channel_id=1, source_target_pairs={{0,3},{1,0},{2,1},{3,2},{4,7},{5,4},{6,5},{7,6},{8,11},{9,8},{10,9... | collective-permute-start | bytes 1179656 | tf_op jit(solution)/shard_map/ppermute | solution.py:343
  14.3 1.6 %collective-permute-start = (bf16[128,1536]{1,0:T(8,128)(2,1)S(1)}, bf16[128,1536]{1,0:T(8,128)(2,1)S(1)}, u32[]{:S(2)}, u32[]{:S(2)}) collective-permute-start(bf16[128,1536]{1,0:T(8,128)(2,1)S(1)} %copy-done.4), channel_id=1, source_target_pairs={{0,2},{1,3},{2,0},{3,1},{4,6},{5,7},{6,4},{7,5},{8,10},{9,11},{10,... | collective-permute-start | bytes 1179656 | tf_op jit(solution)/shard_map/ppermute | solution.py:343
  15.8 0.0 copy-done.6
  15.8 1.2 %collective-permute-start.6 = (bf16[128,768]{1,0:T(8,128)(2,1)S(1)}, bf16[128,768]{1,0:T(8,128)(2,1)S(1)}, u32[]{:S(2)}, u32[]{:S(2)}) collective-permute-start(bf16[128,768]{1,0:T(8,128)(2,1)S(1)} %copy-done.6), channel_id=1, source_target_pairs={{0,8},{8,16},{16,24},{24,0},{1,9},{9,17},{17,25},{25,1},{2,10},{10... | collective-permute-start | bytes 589832 | tf_op jit(solution)/shard_map/ppermute | solution.py:343
  17.1 1.5 %collective-permute-start.8 = (bf16[128,768]{1,0:T(8,128)(2,1)S(1)}, bf16[128,768]{1,0:T(8,128)(2,1)S(1)}, u32[]{:S(2)}, u32[]{:S(2)}) collective-permute-start(bf16[128,768]{1,0:T(8,128)(2,1)S(1)} %copy-done.6), channel_id=1, source_target_pairs={{0,24},{8,0},{16,8},{24,16},{1,25},{9,1},{17,9},{25,17},{2,26},{10... | collective-permute-start | bytes 589832 | tf_op jit(solution)/shard_map/ppermute | solution.py:343
  18.5 3.3 %collective-permute-done.6.refs_1_ = bf16[128,768]{1,0:T(8,128)(2,1)S(1)} collective-permute-done((bf16[128,768]{1,0:T(8,128)(2,1)S(1)}, bf16[128,768]{1,0:T(8,128)(2,1)S(1)}, u32[]{:S(2)}, u32[]{:S(2)}) %collective-permute-start.6) | collective-permute-done | bytes 196640 | tf_op jit(solution)/shard_map/ppermute | solution.py:343
  21.9 0.0 collective-permute-start.7
  21.9 2.0 %tables.1.refs_0_.table = s32[192]{0:T(256)} custom-call(s32[64]{0:T(128)} %pair.1), custom_call_target="tpu_custom_call" | custom-call | flops 1000000 | bytes 1000 | tf_op jit(solution)/shard_map/tables/pallas_call | solution.py:85
  23.9 0.0 copy-start
  23.9 3.7 %copy-done = bf16[768,6144]{1,0:T(8,128)(2,1)S(1)} copy-done((bf16[768,6144]{1,0:T(8,128)(2,1)S(1)}, bf16[768,6144]{1,0:T(8,128)(2,1)}, u32[]{:S(2)}) %copy-start) | copy-done | bytes 9437208
  27.6 0.0 copy-start.1
  27.6 1.0 %copy-done.1 = bf16[8,128,256]{2,1,0:T(8,128)(2,1)S(1)} copy-done((bf16[8,128,256]{2,1,0:T(8,128)(2,1)S(1)}, bf16[8,128,256]{2,1,0:T(8,128)(2,1)}, u32[]{:S(2)}) %copy-start.1) | copy-done | bytes 524312
  28.6 0.0 copy-start.5
  28.6 1.2 %project_own.1 = (f32[768,128]{1,0:T(8,128)S(1)}, bf16[3,768,1536]{2,1,0:T(8,128)(2,1)S(1)}) custom-call(bf16[128,1536]{1,0:T(8,128)(2,1)S(1)} %copy-done.4, bf16[768,6144]{1,0:T(8,128)(2,1)S(1)} %copy-done, bf16[8,128,256]{2,1,0:T(8,128)(2,1)S(1)} %copy-done.1), custom_call_target="tpu_custom_call" | custom-call | flops 300000000 | bytes 1000000 | tf_op jit(solution)/shard_map/project_own/pallas_call | solution.py:291
  29.8 0.0 collective-permute-done.1.one
  29.9 0.0 collective-permute-done.2.three
  29.9 1.4 %project_near.1.sum_ref = f32[768,128]{1,0:T(8,128)S(1)} custom-call(bf16[128,1536]{1,0:T(8,128)(2,1)S(1)} %collective-permute-done.1.one, bf16[128,1536]{1,0:T(8,128)(2,1)S(1)} %collective-permute-done.2.three, bf16[3,768,1536]{2,1,0:T(8,128)(2,1)S(1)} %get-tuple-element.16.rest, f32[768,128]{1,0:T(8,128)S(1)} %get-tuple-element.17.sum_ref), custom_call_target="tpu_custom_call" | custom-call | flops 600000000 | bytes 1000000 | tf_op jit(solution)/shard_map/project_near/pallas_call | solution.py:291
  31.2 0.8 collective-permute-done.part
  32.0 0.0 copy-done.5
  32.0 0.8 project_far.1.refs_0_
  32.9 0.0 collective-permute-done.8.refs_3_
  32.9 0.0 collective-permute-done.7.refs_2_
  32.9 0.6 slice_add_fusion.refs_1_
  33.5 0.0 all-to-all-done.refs_0_
  33.5 0.0 copy-start.2
  33.5 0.8 copy-done.2
  34.3 2.2 %collective-permute-start.9 = (bf16[8,128,256]{2,1,0:T(8,128)(2,1)}, bf16[8,128,256]{2,1,0:T(8,128)(2,1)S(1)}, u32[]{:S(2)}, u32[]{:S(2)}) collective-permute-start(bf16[8,128,256]{2,1,0:T(8,128)(2,1)} %after.1.refs_4_), channel_id=1, source_target_pairs={{0,4},{4,0},{1,5},{5,1},{2,6},{6,2},{3,7},{7,3},{8,12},{12,8},{9,1... | collective-permute-start | bytes 1572872 | tf_op jit(solution)/shard_map/ppermute | solution.py:343
  36.5 1.2 %collective-permute-start.3 = (bf16[128,768]{1,0:T(8,128)(2,1)S(1)}, bf16[128,768]{1,0:T(8,128)(2,1)S(1)}, u32[]{:S(2)}, u32[]{:S(2)}) collective-permute-start(bf16[128,768]{1,0:T(8,128)(2,1)S(1)} %project_far.1.refs_0_), channel_id=1, source_target_pairs={{0,8},{8,16},{16,24},{24,0},{1,9},{9,17},{17,25},{25,1},{2,10},{10... | collective-permute-start | bytes 589832 | tf_op jit(solution)/shard_map/ppermute | solution.py:343
  37.7 2.7 %collective-permute-start.4 = (bf16[128,768]{1,0:T(8,128)(2,1)S(1)}, bf16[128,768]{1,0:T(8,128)(2,1)S(1)}, u32[]{:S(2)}, u32[]{:S(2)}) collective-permute-start(bf16[128,768]{1,0:T(8,128)(2,1)S(1)} %project_far.1.refs_0_), channel_id=1, source_target_pairs={{0,16},{8,24},{16,0},{24,8},{1,17},{9,25},{17,1},{25,9},{2,18},{10... | collective-permute-start | bytes 589832 | tf_op jit(solution)/shard_map/ppermute | solution.py:343
  40.3 0.7 collective-permute-start.5
  41.0 0.0 collective-permute-done.9.refs_5_
  41.0 1.0 %copy-done.3 = bf16[8,128,256]{2,1,0:T(8,128)(2,1)S(1)} copy-done((bf16[8,128,256]{2,1,0:T(8,128)(2,1)S(1)}, bf16[8,128,256]{2,1,0:T(8,128)(2,1)}, u32[]{:S(2)}) %copy-start.3) | copy-done | bytes 524312
  42.1 7.8 %forward.1 = (bf16[2048,256]{1,0:T(8,128)(2,1)S(1)}, bf16[9,384,128]{2,1,0:T(8,128)(2,1)S(1)}, bf16[9,128,384]{2,1,0:T(8,128)(2,1)S(1)}, f32[2,9,8,384]{3,2,1,0:T(8,128)S(1)}, f32[9,128,384]{2,1,0:T(8,128)S(1)}) custom-call(s32[192]{0:T(256)S(1)} %copy-done.5, bf16[128,768]{1,0:T(8,128)(2,1)S(1)} %copy-done.6, ...), custom_call_target="tpu_custom_call" | custom-call | flops 4000000000 | bytes 1000000 | tf_op jit(solution)/shard_map/forward/pallas_call | solution.py:307
  49.8 0.0 collective-permute-done.3.refs_1_
  49.8 0.0 collective-permute-done.4.refs_2_
  49.8 0.0 collective-permute-done.5.refs_3_
  49.8 0.9 weights.1
  50.8 0.9 collective-permute-start.10
  51.6 2.2 %collective-permute-start.11 = (f32[3,8,384]{2,1,0:T(8,128)S(1)}, f32[3,8,384]{2,1,0:T(8,128)S(1)}, u32[]{:S(2)}, u32[]{:S(2)}) collective-permute-start(f32[3,8,384]{2,1,0:T(8,128)S(1)} %get-tuple-element.20.refs_0_), channel_id=1, source_target_pairs={{0,16},{8,24},{16,0},{24,8},{1,17},{9,25},{17,1},{25,9},{2,18},{10... | collective-permute-start | bytes 110600 | tf_op jit(solution)/shard_map/ppermute | solution.py:343
  53.9 0.4 collective-permute-start.12
  54.3 0.6 collective-permute-done.10.refs_1_
  54.9 1.3 %collective-permute-done.11.refs_2_ = f32[3,8,384]{2,1,0:T(8,128)S(1)} collective-permute-done((f32[3,8,384]{2,1,0:T(8,128)S(1)}, f32[3,8,384]{2,1,0:T(8,128)S(1)}, u32[]{:S(2)}, u32[]{:S(2)}) %collective-permute-start.11) | collective-permute-done | bytes 36896 | tf_op jit(solution)/shard_map/ppermute | solution.py:343
  56.1 0.9 collective-permute-done.12.refs_3_
  57.1 11.4 %backward.1 = (f32[128,768]{1,0:T(8,128)S(1)}, bf16[3,128,768]{2,1,0:T(8,128)(2,1)S(1)}, bf16[16,128,256]{2,1,0:T(8,128)(2,1)S(1)}) custom-call(s32[192]{0:T(256)S(1)} %copy-done.5, f32[3,8,384]{2,1,0:T(8,128)S(1)} %get-tuple-element.20.refs_0_, f32[3,8,384]{2,1,0:T(8,128)S(1)} %collective-permute-done.10.refs_1_, ...), custom_call_target="tpu_custom_call" | custom-call | flops 8000000000 | bytes 1000000 | tf_op jit(solution)/shard_map/backward/pallas_call | solution.py:307
  68.5 1.9 %collective-permute-start.16 = (bf16[8,128,256]{2,1,0:T(8,128)(2,1)S(1)}, bf16[8,128,256]{2,1,0:T(8,128)(2,1)S(1)}, u32[]{:S(2)}, u32[]{:S(2)}) collective-permute-start(bf16[8,128,256]{2,1,0:T(8,128)(2,1)S(1)} %slice.43), channel_id=1, source_target_pairs={{0,4},{4,0},{1,5},{5,1},{2,6},{6,2},{3,7},{7,3},{8,12},{12,8},{9,1... | collective-permute-start | bytes 1572872 | tf_op jit(solution)/shard_map/ppermute | solution.py:343
  70.4 1.5 %collective-permute-done.16 = bf16[8,128,256]{2,1,0:T(8,128)(2,1)S(1)} collective-permute-done((bf16[8,128,256]{2,1,0:T(8,128)(2,1)S(1)}, bf16[8,128,256]{2,1,0:T(8,128)(2,1)S(1)}, u32[]{:S(2)}, u32[]{:S(2)}) %collective-permute-start.16) | collective-permute-done | bytes 524320 | tf_op jit(solution)/shard_map/ppermute | solution.py:343
  72.0 0.9 add_convert_fusion
  72.9 6.8 %all-to-all-start.1 = ((bf16[8,128,256]{2,1,0:T(8,128)(2,1)}), bf16[8,128,256]{2,1,0:T(8,128)(2,1)S(1)}, u32[]{:S(2)}, u32[]{:S(2)}) async-start(bf16[8,128,256]{2,1,0:T(8,128)(2,1)} %add_convert_fusion), calls=%async_computation.1 | async-start | bytes 1048576 | tf_op jit(solution)/shard_map/all_to_all | solution.py:413
  79.8 0.7 collective-permute-start.13
  80.4 2.8 %collective-permute-start.14 = (bf16[128,768]{1,0:T(8,128)(2,1)S(1)}, bf16[128,768]{1,0:T(8,128)(2,1)S(1)}, u32[]{:S(2)}, u32[]{:S(2)}) collective-permute-start(bf16[128,768]{1,0:T(8,128)(2,1)S(1)} %get-tuple-element.31), channel_id=1, source_target_pairs={{0,16},{8,24},{16,0},{24,8},{1,17},{9,25},{17,1},{25,9},{2,18},{10... | collective-permute-start | bytes 589832 | tf_op jit(solution)/shard_map/ppermute | solution.py:343
  83.3 0.0 collective-permute-start.15
  83.3 3.6 %collective-permute-done.13 = bf16[128,768]{1,0:T(8,128)(2,1)S(1)} collective-permute-done((bf16[128,768]{1,0:T(8,128)(2,1)S(1)}, bf16[128,768]{1,0:T(8,128)(2,1)S(1)}, u32[]{:S(2)}, u32[]{:S(2)}) %collective-permute-start.13) | collective-permute-done | bytes 196640 | tf_op jit(solution)/shard_map/ppermute | solution.py:343
  86.9 4.9 %collective-permute-done.14 = bf16[128,768]{1,0:T(8,128)(2,1)S(1)} collective-permute-done((bf16[128,768]{1,0:T(8,128)(2,1)S(1)}, bf16[128,768]{1,0:T(8,128)(2,1)S(1)}, u32[]{:S(2)}, u32[]{:S(2)}) %collective-permute-start.14) | collective-permute-done | bytes 196640 | tf_op jit(solution)/shard_map/ppermute | solution.py:343
  91.8 0.0 collective-permute-done.15
  91.8 0.8 convert_add_fusion
  92.6 5.1 %all-to-all-done.1 = bf16[8,128,256]{2,1,0:T(8,128)(2,1)S(1)} async-done(((bf16[8,128,256]{2,1,0:T(8,128)(2,1)}), bf16[8,128,256]{2,1,0:T(8,128)(2,1)S(1)}, u32[]{:S(2)}, u32[]{:S(2)}) %all-to-all-start.1) | async-done | bytes 524320 | tf_op jit(solution)/shard_map/all_to_all | solution.py:413
  97.7 0.1 convert_reduce_fusion
  97.8 0.7 fusion
  (4 shorter events, 0.1 us)
Async XLA Ops:
  0.6 10.8 %copy-start.4 = (bf16[128,1536]{1,0:T(8,128)(2,1)S(1)}, bf16[128,1536]{1,0:T(8,128)(2,1)}, u32[]{:S(2)}) copy-start(bf16[128,1536]{1,0:T(8,128)(2,1)} %own.1) | copy-start | bytes 1179652
  0.6 15.2 %copy-start.6 = (bf16[128,768]{1,0:T(8,128)(2,1)S(1)}, bf16[128,768]{1,0:T(8,128)(2,1)}, u32[]{:S(2)}) copy-start(bf16[128,768]{1,0:T(8,128)(2,1)} %refs_0_.1) | copy-start | bytes 589828
  2.4 31.1 %all-to-all-start = ((bf16[8,128,256]{2,1,0:T(8,128)(2,1)}), bf16[8,128,256]{2,1,0:T(8,128)(2,1)S(1)}, u32[]{:S(2)}, u32[]{:S(2)}) async-start(bf16[8,128,256]{2,1,0:T(8,128)(2,1)} %spread.1.unread), calls=%async_computation | async-start | bytes 1048576 | tf_op jit(solution)/shard_map/all_to_all | solution.py:380
  11.4 18.5 %collective-permute-start.1 = (bf16[128,1536]{1,0:T(8,128)(2,1)S(1)}, bf16[128,1536]{1,0:T(8,128)(2,1)S(1)}, u32[]{:S(2)}, u32[]{:S(2)}) collective-permute-start(bf16[128,1536]{1,0:T(8,128)(2,1)S(1)} %copy-done.4), channel_id=1, source_target_pairs={{0,1},{1,2},{2,3},{3,0},{4,5},{5,6},{6,7},{7,4},{8,9},{9,10},{10,1... | collective-permute-start | bytes 1179656 | tf_op jit(solution)/shard_map/ppermute | solution.py:343
  12.8 17.1 %collective-permute-start.2 = (bf16[128,1536]{1,0:T(8,128)(2,1)S(1)}, bf16[128,1536]{1,0:T(8,128)(2,1)S(1)}, u32[]{:S(2)}, u32[]{:S(2)}) collective-permute-start(bf16[128,1536]{1,0:T(8,128)(2,1)S(1)} %copy-done.4), channel_id=1, source_target_pairs={{0,3},{1,0},{2,1},{3,2},{4,7},{5,4},{6,5},{7,6},{8,11},{9,8},{10,9... | collective-permute-start | bytes 1179656 | tf_op jit(solution)/shard_map/ppermute | solution.py:343
  14.3 17.7 %collective-permute-start = (bf16[128,1536]{1,0:T(8,128)(2,1)S(1)}, bf16[128,1536]{1,0:T(8,128)(2,1)S(1)}, u32[]{:S(2)}, u32[]{:S(2)}) collective-permute-start(bf16[128,1536]{1,0:T(8,128)(2,1)S(1)} %copy-done.4), channel_id=1, source_target_pairs={{0,2},{1,3},{2,0},{3,1},{4,6},{5,7},{6,4},{7,5},{8,10},{9,11},{10,... | collective-permute-start | bytes 1179656 | tf_op jit(solution)/shard_map/ppermute | solution.py:343
  15.8 6.0 %collective-permute-start.6 = (bf16[128,768]{1,0:T(8,128)(2,1)S(1)}, bf16[128,768]{1,0:T(8,128)(2,1)S(1)}, u32[]{:S(2)}, u32[]{:S(2)}) collective-permute-start(bf16[128,768]{1,0:T(8,128)(2,1)S(1)} %copy-done.6), channel_id=1, source_target_pairs={{0,8},{8,16},{16,24},{24,0},{1,9},{9,17},{17,25},{25,1},{2,10},{10... | collective-permute-start | bytes 589832 | tf_op jit(solution)/shard_map/ppermute | solution.py:343
  17.1 15.8 %collective-permute-start.8 = (bf16[128,768]{1,0:T(8,128)(2,1)S(1)}, bf16[128,768]{1,0:T(8,128)(2,1)S(1)}, u32[]{:S(2)}, u32[]{:S(2)}) collective-permute-start(bf16[128,768]{1,0:T(8,128)(2,1)S(1)} %copy-done.6), channel_id=1, source_target_pairs={{0,24},{8,0},{16,8},{24,16},{1,25},{9,1},{17,9},{25,17},{2,26},{10... | collective-permute-start | bytes 589832 | tf_op jit(solution)/shard_map/ppermute | solution.py:343
  21.9 11.0 %collective-permute-start.7 = (bf16[128,768]{1,0:T(8,128)(2,1)S(1)}, bf16[128,768]{1,0:T(8,128)(2,1)S(1)}, u32[]{:S(2)}, u32[]{:S(2)}) collective-permute-start(bf16[128,768]{1,0:T(8,128)(2,1)S(1)} %collective-permute-done.6.refs_1_), channel_id=1, source_target_pairs={{0,8},{8,16},{16,24},{24,0},{1,9},{9,17},{17,25},{25,1},{2,10},{10... | collective-permute-start | bytes 589832 | tf_op jit(solution)/shard_map/ppermute | solution.py:343
  23.9 3.7 %copy-start = (bf16[768,6144]{1,0:T(8,128)(2,1)S(1)}, bf16[768,6144]{1,0:T(8,128)(2,1)}, u32[]{:S(2)}) copy-start(bf16[768,6144]{1,0:T(8,128)(2,1)} %w_ref.1) | copy-start | bytes 28311556
  27.6 1.0 %copy-start.1 = (bf16[8,128,256]{2,1,0:T(8,128)(2,1)S(1)}, bf16[8,128,256]{2,1,0:T(8,128)(2,1)}, u32[]{:S(2)}) copy-start(bf16[8,128,256]{2,1,0:T(8,128)(2,1)} %spread.1.unread) | copy-start | bytes 1572868
  28.6 3.4 %copy-start.5 = (s32[192]{0:T(256)S(1)}, s32[192]{0:T(256)}, u32[]{:S(2)}) copy-start(s32[192]{0:T(256)} %tables.1.refs_0_.table) | copy-start | bytes 2308
  33.5 0.8 copy-start.2
  34.3 6.7 %collective-permute-start.9 = (bf16[8,128,256]{2,1,0:T(8,128)(2,1)}, bf16[8,128,256]{2,1,0:T(8,128)(2,1)S(1)}, u32[]{:S(2)}, u32[]{:S(2)}) collective-permute-start(bf16[8,128,256]{2,1,0:T(8,128)(2,1)} %after.1.refs_4_), channel_id=1, source_target_pairs={{0,4},{4,0},{1,5},{5,1},{2,6},{6,2},{3,7},{7,3},{8,12},{12,8},{9,1... | collective-permute-start | bytes 1572872 | tf_op jit(solution)/shard_map/ppermute | solution.py:343
  36.5 13.3 %collective-permute-start.3 = (bf16[128,768]{1,0:T(8,128)(2,1)S(1)}, bf16[128,768]{1,0:T(8,128)(2,1)S(1)}, u32[]{:S(2)}, u32[]{:S(2)}) collective-permute-start(bf16[128,768]{1,0:T(8,128)(2,1)S(1)} %project_far.1.refs_0_), channel_id=1, source_target_pairs={{0,8},{8,16},{16,24},{24,0},{1,9},{9,17},{17,25},{25,1},{2,10},{10... | collective-permute-start | bytes 589832 | tf_op jit(solution)/shard_map/ppermute | solution.py:343
  37.7 12.1 %collective-permute-start.4 = (bf16[128,768]{1,0:T(8,128)(2,1)S(1)}, bf16[128,768]{1,0:T(8,128)(2,1)S(1)}, u32[]{:S(2)}, u32[]{:S(2)}) collective-permute-start(bf16[128,768]{1,0:T(8,128)(2,1)S(1)} %project_far.1.refs_0_), channel_id=1, source_target_pairs={{0,16},{8,24},{16,0},{24,8},{1,17},{9,25},{17,1},{25,9},{2,18},{10... | collective-permute-start | bytes 589832 | tf_op jit(solution)/shard_map/ppermute | solution.py:343
  40.3 9.5 %collective-permute-start.5 = (bf16[128,768]{1,0:T(8,128)(2,1)S(1)}, bf16[128,768]{1,0:T(8,128)(2,1)S(1)}, u32[]{:S(2)}, u32[]{:S(2)}) collective-permute-start(bf16[128,768]{1,0:T(8,128)(2,1)S(1)} %project_far.1.refs_0_), channel_id=1, source_target_pairs={{0,24},{8,0},{16,8},{24,16},{1,25},{9,1},{17,9},{25,17},{2,26},{10... | collective-permute-start | bytes 589832 | tf_op jit(solution)/shard_map/ppermute | solution.py:343
  41.0 1.0 %copy-start.3 = (bf16[8,128,256]{2,1,0:T(8,128)(2,1)S(1)}, bf16[8,128,256]{2,1,0:T(8,128)(2,1)}, u32[]{:S(2)}) copy-start(bf16[8,128,256]{2,1,0:T(8,128)(2,1)} %after.1.refs_4_) | copy-start | bytes 1572868
  50.8 4.1 %collective-permute-start.10 = (f32[3,8,384]{2,1,0:T(8,128)S(1)}, f32[3,8,384]{2,1,0:T(8,128)S(1)}, u32[]{:S(2)}, u32[]{:S(2)}) collective-permute-start(f32[3,8,384]{2,1,0:T(8,128)S(1)} %get-tuple-element.20.refs_0_), channel_id=1, source_target_pairs={{0,8},{8,16},{16,24},{24,0},{1,9},{9,17},{17,25},{25,1},{2,10},{10... | collective-permute-start | bytes 110600 | tf_op jit(solution)/shard_map/ppermute | solution.py:343
  51.6 4.5 %collective-permute-start.11 = (f32[3,8,384]{2,1,0:T(8,128)S(1)}, f32[3,8,384]{2,1,0:T(8,128)S(1)}, u32[]{:S(2)}, u32[]{:S(2)}) collective-permute-start(f32[3,8,384]{2,1,0:T(8,128)S(1)} %get-tuple-element.20.refs_0_), channel_id=1, source_target_pairs={{0,16},{8,24},{16,0},{24,8},{1,17},{9,25},{17,1},{25,9},{2,18},{10... | collective-permute-start | bytes 110600 | tf_op jit(solution)/shard_map/ppermute | solution.py:343
  53.9 3.2 %collective-permute-start.12 = (f32[3,8,384]{2,1,0:T(8,128)S(1)}, f32[3,8,384]{2,1,0:T(8,128)S(1)}, u32[]{:S(2)}, u32[]{:S(2)}) collective-permute-start(f32[3,8,384]{2,1,0:T(8,128)S(1)} %get-tuple-element.20.refs_0_), channel_id=1, source_target_pairs={{0,24},{8,0},{16,8},{24,16},{1,25},{9,1},{17,9},{25,17},{2,26},{10... | collective-permute-start | bytes 110600 | tf_op jit(solution)/shard_map/ppermute | solution.py:343
  68.5 3.5 %collective-permute-start.16 = (bf16[8,128,256]{2,1,0:T(8,128)(2,1)S(1)}, bf16[8,128,256]{2,1,0:T(8,128)(2,1)S(1)}, u32[]{:S(2)}, u32[]{:S(2)}) collective-permute-start(bf16[8,128,256]{2,1,0:T(8,128)(2,1)S(1)} %slice.43), channel_id=1, source_target_pairs={{0,4},{4,0},{1,5},{5,1},{2,6},{6,2},{3,7},{7,3},{8,12},{12,8},{9,1... | collective-permute-start | bytes 1572872 | tf_op jit(solution)/shard_map/ppermute | solution.py:343
  72.9 24.8 %all-to-all-start.1 = ((bf16[8,128,256]{2,1,0:T(8,128)(2,1)}), bf16[8,128,256]{2,1,0:T(8,128)(2,1)S(1)}, u32[]{:S(2)}, u32[]{:S(2)}) async-start(bf16[8,128,256]{2,1,0:T(8,128)(2,1)} %add_convert_fusion), calls=%async_computation.1 | async-start | bytes 1048576 | tf_op jit(solution)/shard_map/all_to_all | solution.py:413
  79.8 7.1 %collective-permute-start.13 = (bf16[128,768]{1,0:T(8,128)(2,1)S(1)}, bf16[128,768]{1,0:T(8,128)(2,1)S(1)}, u32[]{:S(2)}, u32[]{:S(2)}) collective-permute-start(bf16[128,768]{1,0:T(8,128)(2,1)S(1)} %get-tuple-element.29), channel_id=1, source_target_pairs={{0,8},{8,16},{16,24},{24,0},{1,9},{9,17},{17,25},{25,1},{2,10},{10... | collective-permute-start | bytes 589832 | tf_op jit(solution)/shard_map/ppermute | solution.py:343
  80.4 11.4 %collective-permute-start.14 = (bf16[128,768]{1,0:T(8,128)(2,1)S(1)}, bf16[128,768]{1,0:T(8,128)(2,1)S(1)}, u32[]{:S(2)}, u32[]{:S(2)}) collective-permute-start(bf16[128,768]{1,0:T(8,128)(2,1)S(1)} %get-tuple-element.31), channel_id=1, source_target_pairs={{0,16},{8,24},{16,0},{24,8},{1,17},{9,25},{17,1},{25,9},{2,18},{10... | collective-permute-start | bytes 589832 | tf_op jit(solution)/shard_map/ppermute | solution.py:343
  83.3 8.5 %collective-permute-start.15 = (bf16[128,768]{1,0:T(8,128)(2,1)S(1)}, bf16[128,768]{1,0:T(8,128)(2,1)S(1)}, u32[]{:S(2)}, u32[]{:S(2)}) collective-permute-start(bf16[128,768]{1,0:T(8,128)(2,1)S(1)} %get-tuple-element.30), channel_id=1, source_target_pairs={{0,24},{8,0},{16,8},{24,16},{1,25},{9,1},{17,9},{25,17},{2,26},{10... | collective-permute-start | bytes 589832 | tf_op jit(solution)/shard_map/ppermute | solution.py:343
